TPU v7x, 256 devices: a whole 4x4x8 slice. The times are simulated.
256 devices in a mesh: tm: 8 (over x, core), gx: 8 (over z), gy: 4 (over y).
Axes of the slice: x: 4, y: 4, z: 8, core: 2. Of those that a mesh axis runs over, the one named last changes fastest.
Arguments:
- initial_drop: float32 [512, 4096], P('gx', 'gy'), may hold values from -6 to 6
- guess_c: float32 [8, 512, 4096], P('tm', 'gx', 'gy'), may hold values from -6 to 6
- class_map: int32 [512, 4096], P('gx', 'gy'), may hold values from 0 to 7
- class_conductance: float32 [8], replicated, may hold values from 0.25 to 2
- capacitance: float32 [512, 4096], P('gx', 'gy'), may hold values from 1 to 8
- base_current: float32 [512, 4096], P('gx', 'gy'), may hold values from 0.05 to 0.5
- tap_index: int32 [32, 512, 4096], P('tm', 'gx', 'gy'), may hold values from 0 to 3
- tap_levels: float32 [4], replicated, may hold values from 0.25 to 2
Outputs:
- corrected: float32 [8, 512, 4096], P('tm', 'gx', 'gy')
- coarse_residual: float32 [8, 512, 4096], P('tm', 'gx', 'gy')
All inputs are finite; a program needn't handle non-finite values.
Results may differ from a plain program's by a relative error of at most 0.00002.
Values sent between devices are 32-bit elements; how exact they have to be, the bound alone decides.
A program may use at most 64 MiB of HBM per device.

v0:
```python
import jax
import jax.numpy as jnp
from jax import lax
from jax.sharding import PartitionSpec as P

GROUP_STEPS = 4
SWEEPS = 4
NCLS = 8
NLEV = 4


RHO = 0.9


def with_halo(block, sides, width):
    for axis, dim in sides:
        count = lax.axis_size(axis)
        forward = [(i, i + 1) for i in range(count - 1)]
        backward = [(target, source) for source, target in forward]
        low = lax.ppermute(
            lax.slice_in_dim(block, block.shape[dim] - width, None, axis=dim), axis, forward
        )
        high = lax.ppermute(lax.slice_in_dim(block, 0, width, axis=dim), axis, backward)
        block = jnp.concatenate([low, block, high], axis=dim)
    return block


def shifted(value, axis, steps):
    count = lax.axis_size(axis)
    pairs = [(source, (source + steps) % count) for source in range(count)]
    return lax.ppermute(value, axis, pairs)


def passed_along(block, axis, distance):
    devices = range(lax.axis_size(axis))
    route = [(i - distance, i) for i in devices if i - distance in devices]
    return lax.ppermute(block, axis, route)


def cheb_weights(sweep_total):
    weights = [1.0]
    while len(weights) < sweep_total:
        if len(weights) == 1:
            weights.append(1.0 / (1.0 - RHO * RHO / 2.0))
        else:
            weights.append(1.0 / (1.0 - RHO * RHO * weights[-1] / 4.0))
    return weights


def table_field(index_map, table, table_size):
    result = jnp.zeros(index_map.shape, jnp.float32)
    for level_no in range(table_size):
        result = result + jnp.where(index_map == level_no, table[level_no], 0.0)
    return result


def shards(
    initial_drop,
    guess_c,
    class_map,
    class_conductance,
    capacitance,
    base_current,
    tap_index,
    tap_levels,
):
    group_id = lax.axis_index("tm")
    node_conductance = table_field(class_map, class_conductance, NCLS)
    node_fields = jnp.stack([node_conductance, capacitance, jnp.ones_like(capacitance)])
    node_wide = with_halo(node_fields, (("gx", 1), ("gy", 2)), 1)
    wide_kappa = node_wide[0]
    east_west = 0.5 * (wide_kappa[:-1, 1:-1] + wide_kappa[1:, 1:-1])
    south_north = 0.5 * (wide_kappa[1:-1, :-1] + wide_kappa[1:-1, 1:])
    cap_region = node_wide[1, 1:-1, 1:-1]
    inside = node_wide[2, 1:-1, 1:-1] > 0.5
    diag_fine = (
        cap_region + east_west[:-1] + east_west[1:] + south_north[:, :-1] + south_north[:, 1:]
    )
    cap_region_coarse = cap_region / GROUP_STEPS
    diag_coarse = (
        cap_region_coarse
        + east_west[:-1]
        + east_west[1:]
        + south_north[:, :-1]
        + south_north[:, 1:]
    )
    inv_fine = jnp.where(inside, 1.0 / jnp.where(inside, diag_fine, 1.0), 0.0)
    inv_coarse = jnp.where(inside, 1.0 / jnp.where(inside, diag_coarse, 1.0), 0.0)
    cap_coarse = capacitance / GROUP_STEPS
    weights = cheb_weights(SWEEPS)

    def sweep_once(current, source, inverse):
        beside = (
            east_west[:-1] * current[:-2, 1:-1]
            + east_west[1:] * current[2:, 1:-1]
            + south_north[:, :-1] * current[1:-1, :-2]
            + south_north[:, 1:] * current[1:-1, 2:]
        )
        return inverse * (source + beside)

    def chebyshev(start_v, source, inverse):
        previous = start_v
        current = start_v
        for weight in weights:
            padded = with_halo(current, (("gx", 0), ("gy", 1)), 1)
            jacobi = sweep_once(padded, source, inverse)
            newest = weight * (jacobi - previous) + previous
            previous = current
            current = newest
        return current

    def fine_step(start_v, step_no):
        load_now = base_current * table_field(tap_index[step_no], tap_levels, NLEV)
        return chebyshev(start_v, capacitance * start_v + load_now, inv_fine)

    def coarse_step(start_v):
        return chebyshev(start_v, cap_coarse * start_v, inv_coarse)

    def relax_f(start_v):
        state_now = start_v
        for step_no in range(GROUP_STEPS - 1):
            state_now = fine_step(state_now, step_no)
        return state_now

    first_zone = group_id == 0
    prior_c = shifted(guess_c, "tm", 1)[0]
    relaxed_c = fine_step(relax_f(prior_c), GROUP_STEPS - 1)
    before = passed_along(relaxed_c[None], "tm", 1)[0]
    residual = (
        fine_step(relax_f(jnp.where(first_zone, initial_drop, before)), GROUP_STEPS - 1) - relaxed_c
    )
    chain_len = lax.axis_size("tm")

    def chain_round(round_no, error_now):
        earlier = passed_along(error_now[None], "tm", 1)[0]
        return coarse_step(earlier) + residual

    correction = lax.fori_loop(0, chain_len, chain_round, jnp.zeros_like(residual))
    return ((relaxed_c + correction)[None], residual[None])


def solution(mesh):
    placed = (
        P("gx", "gy"),
        P("tm", "gx", "gy"),
        P("gx", "gy"),
        P(),
        P("gx", "gy"),
        P("gx", "gy"),
        P("tm", "gx", "gy"),
        P(),
    )
    return jax.shard_map(
        shards,
        mesh=mesh,
        in_specs=placed,
        out_specs=(P("tm", "gx", "gy"), P("tm", "gx", "gy")),
        check_vma=False,
    )
```

profile of v0, /device:TPU:77, one launch (start us, length us, event | category | flops | bytes accessed | tf_op | source)
XLA Modules:
  0.0 1213.8 jit_solution(4304944235646490926)
XLA Ops:
  2.3 6.1 add_bitcast_fusion.1
  277.4 41.7 %collective-permute-start.86 = (f32[1,64,1024]{2,1,0:T(8,128)S(1)}, f32[1,64,1024]{2,1,0:T(8,128)S(1)}, u32[]{:S(2)}, u32[]{:S(2)}) collective-permute-start(f32[1,64,1024]{2,1,0:T(8,128)S(1)} %bitcast.88), channel_id=1, source_target_pairs={{0,32},{32,64},{64,96},{96,128},{128,160},{160,192},{192,224},{1,3... | collective-permute-start | bytes 786440 | tf_op jit(solution)/shard_map/ppermute | solution.py:37
  559.6 653.3 %while.11 = (s32[]{:T(128)}, f32[64,1024]{1,0:T(8,128)S(1)}, f32[64,1024]{1,0:T(8,128)S(1)}, f32[65,1024]{1,0:T(8,128)S(1)}, f32[64,1025]{1,0:T(8,128)S(1)}, /*i...) while((s32[]{:T(128)}, f32[64,1024]{1,0:T(8,128)S(1)}, ...), condition=%wide.region_1.2_spmd.clone, body=%wide.region_0.1_spmd.clone.sunk | while | flops 5571619 | bytes 13120655 | solution.py:138
  559.7 40.8 %collective-permute-start = (f32[1,64,1024]{2,1,0:T(8,128)S(1)}, f32[1,64,1024]{2,1,0:T(8,128)S(1)}, u32[]{:S(2)}, u32[]{:S(2)}) collective-permute-start(f32[1,64,1024]{2,1,0:T(8,128)S(1)} %select_bitcast_fusion.2), channel_id=1, source_target_pairs={{0,32},{32,64},{64,96},{96,128},{128,160},{160,192},{192,224},{1,3... | collective-permute-start | bytes 786440 | tf_op jit(solution)/shard_map/while/body/eval_jaxpr/ppermute | solution.py:37
  664.7 13.8 %collective-permute-start = (f32[1,64,1024]{2,1,0:T(8,128)S(1)}, f32[1,64,1024]{2,1,0:T(8,128)S(1)}, u32[]{:S(2)}, u32[]{:S(2)}) collective-permute-start(f32[1,64,1024]{2,1,0:T(8,128)S(1)} %select_bitcast_fusion.2), channel_id=1, source_target_pairs={{0,32},{32,64},{64,96},{96,128},{128,160},{160,192},{192,224},{1,3... | collective-permute-start | bytes 786440 | tf_op jit(solution)/shard_map/while/body/eval_jaxpr/ppermute | solution.py:37
  683.7 4.9 collective-permute-start.2
  698.3 5.1 collective-permute-start.6
  711.2 4.8 collective-permute-start.10
  743.2 13.6 %collective-permute-start = (f32[1,64,1024]{2,1,0:T(8,128)S(1)}, f32[1,64,1024]{2,1,0:T(8,128)S(1)}, u32[]{:S(2)}, u32[]{:S(2)}) collective-permute-start(f32[1,64,1024]{2,1,0:T(8,128)S(1)} %select_bitcast_fusion.2), channel_id=1, source_target_pairs={{0,32},{32,64},{64,96},{96,128},{128,160},{160,192},{192,224},{1,3... | collective-permute-start | bytes 786440 | tf_op jit(solution)/shard_map/while/body/eval_jaxpr/ppermute | solution.py:37
  762.0 4.9 collective-permute-start.2
  776.6 5.1 collective-permute-start.6
  789.5 4.8 collective-permute-start.10
  821.5 13.6 %collective-permute-start = (f32[1,64,1024]{2,1,0:T(8,128)S(1)}, f32[1,64,1024]{2,1,0:T(8,128)S(1)}, u32[]{:S(2)}, u32[]{:S(2)}) collective-permute-start(f32[1,64,1024]{2,1,0:T(8,128)S(1)} %select_bitcast_fusion.2), channel_id=1, source_target_pairs={{0,32},{32,64},{64,96},{96,128},{128,160},{160,192},{192,224},{1,3... | collective-permute-start | bytes 786440 | tf_op jit(solution)/shard_map/while/body/eval_jaxpr/ppermute | solution.py:37
  840.3 4.9 collective-permute-start.2
  854.9 5.1 collective-permute-start.6
  867.8 4.8 collective-permute-start.10
  899.8 13.6 %collective-permute-start = (f32[1,64,1024]{2,1,0:T(8,128)S(1)}, f32[1,64,1024]{2,1,0:T(8,128)S(1)}, u32[]{:S(2)}, u32[]{:S(2)}) collective-permute-start(f32[1,64,1024]{2,1,0:T(8,128)S(1)} %select_bitcast_fusion.2), channel_id=1, source_target_pairs={{0,32},{32,64},{64,96},{96,128},{128,160},{160,192},{192,224},{1,3... | collective-permute-start | bytes 786440 | tf_op jit(solution)/shard_map/while/body/eval_jaxpr/ppermute | solution.py:37
  918.6 4.9 collective-permute-start.2
  933.2 5.1 collective-permute-start.6
  946.1 4.8 collective-permute-start.10
  978.1 13.6 %collective-permute-start = (f32[1,64,1024]{2,1,0:T(8,128)S(1)}, f32[1,64,1024]{2,1,0:T(8,128)S(1)}, u32[]{:S(2)}, u32[]{:S(2)}) collective-permute-start(f32[1,64,1024]{2,1,0:T(8,128)S(1)} %select_bitcast_fusion.2), channel_id=1, source_target_pairs={{0,32},{32,64},{64,96},{96,128},{128,160},{160,192},{192,224},{1,3... | collective-permute-start | bytes 786440 | tf_op jit(solution)/shard_map/while/body/eval_jaxpr/ppermute | solution.py:37
  996.9 4.9 collective-permute-start.2
  1011.5 5.1 collective-permute-start.6
  1024.4 4.8 collective-permute-start.10
  1056.4 13.6 %collective-permute-start = (f32[1,64,1024]{2,1,0:T(8,128)S(1)}, f32[1,64,1024]{2,1,0:T(8,128)S(1)}, u32[]{:S(2)}, u32[]{:S(2)}) collective-permute-start(f32[1,64,1024]{2,1,0:T(8,128)S(1)} %select_bitcast_fusion.2), channel_id=1, source_target_pairs={{0,32},{32,64},{64,96},{96,128},{128,160},{160,192},{192,224},{1,3... | collective-permute-start | bytes 786440 | tf_op jit(solution)/shard_map/while/body/eval_jaxpr/ppermute | solution.py:37
  1075.2 4.9 collective-permute-start.2
  1089.8 5.1 collective-permute-start.6
  1102.7 4.8 collective-permute-start.10
  1134.7 13.6 %collective-permute-start = (f32[1,64,1024]{2,1,0:T(8,128)S(1)}, f32[1,64,1024]{2,1,0:T(8,128)S(1)}, u32[]{:S(2)}, u32[]{:S(2)}) collective-permute-start(f32[1,64,1024]{2,1,0:T(8,128)S(1)} %select_bitcast_fusion.2), channel_id=1, source_target_pairs={{0,32},{32,64},{64,96},{96,128},{128,160},{160,192},{192,224},{1,3... | collective-permute-start | bytes 786440 | tf_op jit(solution)/shard_map/while/body/eval_jaxpr/ppermute | solution.py:37
  1153.5 4.9 collective-permute-start.2
  1168.1 5.1 collective-permute-start.6
  1181.0 4.8 collective-permute-start.10
  (738 shorter events, 921.3 us)
Async XLA Ops:
  9.4 7.5 collective-permute-start.17
  15.0 14.2 %collective-permute-start.21 = (f32[1,64,1024]{2,1,0:T(8,128)S(1)}, f32[1,64,1024]{2,1,0:T(8,128)S(1)}, u32[]{:S(2)}, u32[]{:S(2)}) collective-permute-start(f32[1,64,1024]{2,1,0:T(8,128)S(1)} %copy-done.6), channel_id=1, source_target_pairs={{0,32},{32,64},{64,96},{96,128},{128,160},{160,192},{192,224},{224... | collective-permute-start | bytes 786440 | tf_op jit(solution)/shard_map/ppermute | solution.py:31
  277.4 45.0 %collective-permute-start.86 = (f32[1,64,1024]{2,1,0:T(8,128)S(1)}, f32[1,64,1024]{2,1,0:T(8,128)S(1)}, u32[]{:S(2)}, u32[]{:S(2)}) collective-permute-start(f32[1,64,1024]{2,1,0:T(8,128)S(1)} %bitcast.88), channel_id=1, source_target_pairs={{0,32},{32,64},{64,96},{96,128},{128,160},{160,192},{192,224},{1,3... | collective-permute-start | bytes 786440 | tf_op jit(solution)/shard_map/ppermute | solution.py:37
  559.7 44.1 %collective-permute-start = (f32[1,64,1024]{2,1,0:T(8,128)S(1)}, f32[1,64,1024]{2,1,0:T(8,128)S(1)}, u32[]{:S(2)}, u32[]{:S(2)}) collective-permute-start(f32[1,64,1024]{2,1,0:T(8,128)S(1)} %select_bitcast_fusion.2), channel_id=1, source_target_pairs={{0,32},{32,64},{64,96},{96,128},{128,160},{160,192},{192,224},{1,3... | collective-permute-start | bytes 786440 | tf_op jit(solution)/shard_map/while/body/eval_jaxpr/ppermute | solution.py:37
  664.7 17.2 %collective-permute-start = (f32[1,64,1024]{2,1,0:T(8,128)S(1)}, f32[1,64,1024]{2,1,0:T(8,128)S(1)}, u32[]{:S(2)}, u32[]{:S(2)}) collective-permute-start(f32[1,64,1024]{2,1,0:T(8,128)S(1)} %select_bitcast_fusion.2), channel_id=1, source_target_pairs={{0,32},{32,64},{64,96},{96,128},{128,160},{160,192},{192,224},{1,3... | collective-permute-start | bytes 786440 | tf_op jit(solution)/shard_map/while/body/eval_jaxpr/ppermute | solution.py:37
  681.8 6.8 collective-permute-start.1
  696.4 7.1 collective-permute-start.5
  711.2 6.8 collective-permute-start.10
  743.2 16.9 %collective-permute-start = (f32[1,64,1024]{2,1,0:T(8,128)S(1)}, f32[1,64,1024]{2,1,0:T(8,128)S(1)}, u32[]{:S(2)}, u32[]{:S(2)}) collective-permute-start(f32[1,64,1024]{2,1,0:T(8,128)S(1)} %select_bitcast_fusion.2), channel_id=1, source_target_pairs={{0,32},{32,64},{64,96},{96,128},{128,160},{160,192},{192,224},{1,3... | collective-permute-start | bytes 786440 | tf_op jit(solution)/shard_map/while/body/eval_jaxpr/ppermute | solution.py:37
  760.1 6.8 collective-permute-start.1
  774.7 7.1 collective-permute-start.5
  789.5 6.8 collective-permute-start.10
  821.5 16.9 %collective-permute-start = (f32[1,64,1024]{2,1,0:T(8,128)S(1)}, f32[1,64,1024]{2,1,0:T(8,128)S(1)}, u32[]{:S(2)}, u32[]{:S(2)}) collective-permute-start(f32[1,64,1024]{2,1,0:T(8,128)S(1)} %select_bitcast_fusion.2), channel_id=1, source_target_pairs={{0,32},{32,64},{64,96},{96,128},{128,160},{160,192},{192,224},{1,3... | collective-permute-start | bytes 786440 | tf_op jit(solution)/shard_map/while/body/eval_jaxpr/ppermute | solution.py:37
  838.4 6.8 collective-permute-start.1
  853.0 7.1 collective-permute-start.5
  867.8 6.8 collective-permute-start.10
  899.8 16.9 %collective-permute-start = (f32[1,64,1024]{2,1,0:T(8,128)S(1)}, f32[1,64,1024]{2,1,0:T(8,128)S(1)}, u32[]{:S(2)}, u32[]{:S(2)}) collective-permute-start(f32[1,64,1024]{2,1,0:T(8,128)S(1)} %select_bitcast_fusion.2), channel_id=1, source_target_pairs={{0,32},{32,64},{64,96},{96,128},{128,160},{160,192},{192,224},{1,3... | collective-permute-start | bytes 786440 | tf_op jit(solution)/shard_map/while/body/eval_jaxpr/ppermute | solution.py:37
  916.7 6.8 collective-permute-start.1
  931.3 7.1 collective-permute-start.5
  946.1 6.8 collective-permute-start.10
  978.1 16.9 %collective-permute-start = (f32[1,64,1024]{2,1,0:T(8,128)S(1)}, f32[1,64,1024]{2,1,0:T(8,128)S(1)}, u32[]{:S(2)}, u32[]{:S(2)}) collective-permute-start(f32[1,64,1024]{2,1,0:T(8,128)S(1)} %select_bitcast_fusion.2), channel_id=1, source_target_pairs={{0,32},{32,64},{64,96},{96,128},{128,160},{160,192},{192,224},{1,3... | collective-permute-start | bytes 786440 | tf_op jit(solution)/shard_map/while/body/eval_jaxpr/ppermute | solution.py:37
  995.0 6.8 collective-permute-start.1
  1009.6 7.1 collective-permute-start.5
  1024.4 6.8 collective-permute-start.10
  1056.4 16.9 %collective-permute-start = (f32[1,64,1024]{2,1,0:T(8,128)S(1)}, f32[1,64,1024]{2,1,0:T(8,128)S(1)}, u32[]{:S(2)}, u32[]{:S(2)}) collective-permute-start(f32[1,64,1024]{2,1,0:T(8,128)S(1)} %select_bitcast_fusion.2), channel_id=1, source_target_pairs={{0,32},{32,64},{64,96},{96,128},{128,160},{160,192},{192,224},{1,3... | collective-permute-start | bytes 786440 | tf_op jit(solution)/shard_map/while/body/eval_jaxpr/ppermute | solution.py:37
  1073.3 6.8 collective-permute-start.1
  1087.9 7.1 collective-permute-start.5
  1102.7 6.8 collective-permute-start.10
  1134.7 16.9 %collective-permute-start = (f32[1,64,1024]{2,1,0:T(8,128)S(1)}, f32[1,64,1024]{2,1,0:T(8,128)S(1)}, u32[]{:S(2)}, u32[]{:S(2)}) collective-permute-start(f32[1,64,1024]{2,1,0:T(8,128)S(1)} %select_bitcast_fusion.2), channel_id=1, source_target_pairs={{0,32},{32,64},{64,96},{96,128},{128,160},{160,192},{192,224},{1,3... | collective-permute-start | bytes 786440 | tf_op jit(solution)/shard_map/while/body/eval_jaxpr/ppermute | solution.py:37
  1151.6 6.8 collective-permute-start.1
  1166.1 7.1 collective-permute-start.5
  1181.0 6.8 collective-permute-start.10
  (245 other events, 1310.9 us)
where the time goes:
time: 1240 us; the launch traced here: 1210 us
  starting transfers between devices  922 us (74%)
  waiting for transfers between devices  237 us (19%)
  other arithmetic  44.9 us (4%)
    ppermute x130, starting transfers between devices, with_halo(): lax.ppermute(lax.slice_in_dim(block, block.shape[dim] - width, None, axis...  438 us
    ppermute x130, starting transfers between devices, with_halo(): lax.ppermute(lax.slice_in_dim(block, 0, width, axis=dim), axis, backward)  305 us
    ppermute x9, starting transfers between devices, passed_along(): return lax.ppermute(block, axis, route)  178 us
    ppermute x130, waiting for transfers between devices, with_halo(): lax.ppermute(lax.slice_in_dim(block, 0, width, axis=dim), axis, backward)  151 us
    ppermute x130, waiting for transfers between devices, with_halo(): lax.ppermute(lax.slice_in_dim(block, block.shape[dim] - width, None, axis...  56.4 us
    ppermute x9, waiting for transfers between devices, passed_along(): return lax.ppermute(block, axis, route)  29.6 us
    add x55, other arithmetic, chebyshev(): newest = weight * (jacobi - previous) + previous  29.6 us
  transfers between devices with their start and end apart: 270, of which 139 were waited for; matrix products, arithmetic and copies ran while one was open for 0% of the time, Pallas kernels for 0%

commit v1 on v0

v1 whole, which is shorter than its diff:
```python
import functools

import jax
import jax.numpy as jnp
from jax import lax
from jax.experimental import pallas as pl
from jax.experimental.pallas import tpu as pltpu
from jax.sharding import PartitionSpec as P

GROUP_STEPS = 4
SWEEPS = 4
NCLS = 8
NLEV = 4
RHO = 0.9

LANES = 128
HALF = 64
ROWS = 64
TILES = 8
WRAP = TILES
ALL = TILES + 1
HALO = 16
GUARD = 8
TOP = GUARD + HALO
END = TOP + ROWS
TALL = END + HALO + GUARD

CHALO = 32
CTOP = GUARD + CHALO
CEND = CTOP + ROWS
CTALL = CEND + CHALO + GUARD

MESH = pl.DeviceIdType.MESH


def cheb_weights(sweep_total):
    weights = [1.0]
    while len(weights) < sweep_total:
        if len(weights) == 1:
            weights.append(1.0 / (1.0 - RHO * RHO / 2.0))
        else:
            weights.append(1.0 / (1.0 - RHO * RHO * weights[-1] / 4.0))
    return weights


def strip(k):
    return -(-(SWEEPS * (TILES - 1 - k)) // 8) * 8


def lane_no():
    return lax.broadcasted_iota(jnp.int32, (8, LANES), 1)


def beside_lanes(tiles, c):
    lane = lane_no()
    n = len(tiles)
    left = pltpu.roll(jnp.where(lane == LANES - 1, tiles[c - 1], tiles[c]), 1, 1)
    right = pltpu.roll(jnp.where(lane == 0, tiles[(c + 1) % n], tiles[c]), LANES - 1, 1)
    return left, right


def sweep(edges, held, scale, load, cur, prev, dst, weight, rows_of, tiles, after=None):
    first = scale is not None
    for r in rows_of:
        rows = pl.ds(r, 8)
        here = [cur[c, rows, :] for c in range(tiles)]
        for c in range(tiles):
            left, right = beside_lanes(here, c)
            up = cur[c, pl.ds(r - 1, 8), :]
            down = cur[c, pl.ds(r + 1, 8), :]
            if first:
                base = scale[c, rows, :] * here[c]
                if load is not None:
                    base = base + load[c, rows, :]
                held[c, rows, :] = base
            else:
                base = held[c, rows, :]
            new = base + (
                (edges[0, c, rows, :] * up + edges[1, c, rows, :] * down)
                + (edges[2, c, rows, :] * left + edges[3, c, rows, :] * right)
            )
            if not first:
                before = prev[c, rows, :]
                new = weight * (new - before) + before
            if after is None:
                dst[c, rows, :] = new
            else:
                after(c, r, new)


def coefficients(kappa, cap, divide, inside, rows_of, tiles, put):
    for r in rows_of:
        rows = pl.ds(r, 8)
        here = [kappa[c, rows, :] for c in range(tiles)]
        for c in range(tiles):
            left, right = beside_lanes(here, c)
            west = 0.5 * (kappa[c, pl.ds(r - 1, 8), :] + here[c])
            east = 0.5 * (here[c] + kappa[c, pl.ds(r + 1, 8), :])
            south = 0.5 * (left + here[c])
            north = 0.5 * (here[c] + right)
            size = cap[c, rows, :] * (1.0 / divide)
            diag = size + west + east + south + north
            ok = inside(c, r)
            inverse = jnp.where(ok, 1.0 / jnp.where(ok, diag, 1.0), 0.0)
            put(c, rows, inverse, size, (west, east, south, north))


def kernel(
    sizes,
    initial_hbm, guess_hbm, class_hbm, conductance, cap_hbm, base_hbm, tap_hbm, levels,
    corrected_hbm, residual_hbm,
    raw, raw_index, field, own, beside, start, work, held, edges, scale, loads,
    relaxed, residual, box, arrived, kc, kc_box, cedges, cscale, cheld, chain, chain_work,
    out_box, error, result,
    in_sem, out_sem, local_sem, send, recv, a2a_send, a2a_recv, back_send, back_recv,
):
    n_tm, n_gx, n_gy = sizes
    me = lax.axis_index("tm")
    gx = lax.axis_index("gx")
    gy = lax.axis_index("gy")
    weights = cheb_weights(SWEEPS)
    lane = lane_no()
    has_up, has_down = gx > 0, gx < n_gx - 1
    has_left, has_right = gy > 0, gy < n_gy - 1
    later = lax.rem(me + 1, n_tm)

    loads_in = [
        pltpu.make_async_copy(guess_hbm.at[0], raw.at[0], in_sem.at[0]),
        pltpu.make_async_copy(class_hbm, raw_index.at[0], in_sem.at[1]),
        pltpu.make_async_copy(cap_hbm, raw.at[1], in_sem.at[2]),
        pltpu.make_async_copy(base_hbm, raw.at[2], in_sem.at[3]),
        pltpu.make_async_copy(tap_hbm, raw_index.at[pl.ds(1, GROUP_STEPS)], in_sem.at[4]),
        pltpu.make_async_copy(initial_hbm, raw.at[3], in_sem.at[5]),
    ]
    for copy in loads_in:
        copy.start()

    def clear(ref, lead, tall, top, end):
        zero = jnp.zeros((8, LANES), jnp.float32)
        for r in list(range(0, top, 8)) + list(range(end, tall, 8)):
            for c in range(ref.shape[len(lead)]):
                ref[lead + (c, pl.ds(r, 8), slice(None))] = zero

    def clear_fields(f, _):
        clear(field, (f,), TALL, TOP, END)
        return 0

    lax.fori_loop(0, 2 + GROUP_STEPS, clear_fields, 0)

    def clear_starts(p, _):
        clear(start, (p,), TALL, TOP, END)
        clear(kc, (p,), CTALL, CTOP, CEND)
        return 0

    lax.fori_loop(0, 2, clear_starts, 0)
    clear(work, (), TALL, TOP, END)
    clear(chain_work, (), CTALL, CTOP, CEND)

    def clear_arrived(k, _):
        clear(arrived, (k,), CTALL, CTOP, CEND)
        return 0

    lax.fori_loop(0, n_tm, clear_arrived, 0)

    barrier = pltpu.get_barrier_semaphore()

    def greet(t, x, y):
        pl.semaphore_signal(barrier, inc=1, device_id=(t, x, y), device_id_type=MESH)

    for d in range(n_tm):
        t = lax.rem(me + d, n_tm)
        if d:
            greet(t, gx, gy)
        pl.when(has_up)(lambda t=t: greet(t, gx - 1, gy))
        pl.when(has_down)(lambda t=t: greet(t, gx + 1, gy))
    pl.when(has_left)(lambda: greet(me, gx, gy - 1))
    pl.when(has_right)(lambda: greet(me, gx, gy + 1))
    one = lambda flag: flag.astype(jnp.int32)
    friends = n_tm * (1 + one(has_up) + one(has_down)) - 1 + one(has_left) + one(has_right)
    pl.semaphore_wait(barrier, friends)

    started = []

    def remote(src, dst, no, device, sends=None, receives=None):
        copy = pltpu.make_async_remote_copy(
            src_ref=src,
            dst_ref=dst,
            send_sem=send.at[no],
            recv_sem=recv.at[no],
            device_id=device,
            device_id_type=MESH,
        )
        if sends is None:
            copy.start()
        else:
            pl.when(sends)(copy.start)
        started.append((copy, sends))

        def wait():
            if receives is None:
                copy.wait_recv()
            else:
                pl.when(receives)(copy.wait_recv)

        return wait

    def shift_on(source, target, lo, count, no):
        part = pl.ds(lo, count)
        return [
            remote(source.at[part], target.at[part, pl.ds(TOP, ROWS)], no, (later, gx, gy)),
            remote(
                source.at[part, pl.ds(0, HALO)],
                target.at[part, pl.ds(END, HALO)],
                no + 1, (later, gx - 1, gy), has_up, has_down,
            ),
            remote(
                source.at[part, pl.ds(ROWS - HALO, HALO)],
                target.at[part, pl.ds(GUARD, HALO)],
                no + 2, (later, gx + 1, gy), has_down, has_up,
            ),
        ]

    def rows_beside(lo, count, no):
        part = pl.ds(lo, count)
        every = pl.ds(0, 2 + GROUP_STEPS)
        return [
            remote(
                field.at[every, part, pl.ds(TOP, HALO)],
                field.at[every, part, pl.ds(END, HALO)],
                no, (me, gx - 1, gy), has_up, has_down,
            ),
            remote(
                field.at[every, part, pl.ds(END - HALO, HALO)],
                field.at[every, part, pl.ds(GUARD, HALO)],
                no + 1, (me, gx + 1, gy), has_down, has_up,
            ),
        ]

    def by_rows(body):
        def run(i, _):
            body(pl.multiple_of(i * 8, 8))
            return 0

        lax.fori_loop(0, ROWS // 8, run, 0)

    def columns(c):
        return slice(c * LANES, (c + 1) * LANES)

    loads_in[0].wait()

    def take_guess(r):
        for c in range(TILES):
            own[0, c, pl.ds(r, 8), :] = raw[0, pl.ds(r, 8), columns(c)]

    by_rows(take_guess)
    wait_start = shift_on(own.at[0], start.at[0], 0, TILES, 0)

    for copy in loads_in[1:]:
        copy.wait()

    def take_fields(r):
        rows, there = pl.ds(r, 8), pl.ds(pl.multiple_of(r + TOP, 8), 8)
        for c in range(TILES):
            kind = raw_index[0, rows, columns(c)]
            kappa = jnp.full((8, LANES), conductance[0], jnp.float32)
            for j in range(1, NCLS):
                kappa = jnp.where(kind == j, conductance[j], kappa)
            field[0, c, there, :] = kappa
            field[1, c, there, :] = raw[1, rows, columns(c)]
            peak = raw[2, rows, columns(c)]
            for n in range(GROUP_STEPS):
                tap = raw_index[1 + n, rows, columns(c)]
                level = jnp.full((8, LANES), levels[0], jnp.float32)
                for j in range(1, NLEV):
                    level = jnp.where(tap == j, levels[j], level)
                field[2 + n, c, there, :] = peak * level
            own[1, c, rows, :] = raw[3, rows, columns(c)]

    by_rows(take_fields)

    fields = pl.ds(0, 2 + GROUP_STEPS)
    mid = pl.ds(TOP, ROWS)
    owns = pl.ds(2 + GROUP_STEPS, 2)
    wait_lanes = [
        remote(field.at[fields, 0, mid], beside.at[0, fields], 6,
               (me, gx, gy - 1), has_left, has_right),
        remote(own.at[pl.ds(0, 2), 0], beside.at[0, owns], 7,
               (me, gx, gy - 1), has_left, has_right),
        remote(field.at[fields, TILES - 1, mid], beside.at[1, fields], 8,
               (me, gx, gy + 1), has_right, has_left),
        remote(own.at[pl.ds(0, 2), TILES - 1], beside.at[1, owns], 9,
               (me, gx, gy + 1), has_right, has_left),
    ]
    wait_rows = rows_beside(0, TILES, 10)

    def blank(side):
        def run():
            def body(f, _):
                beside[side, f] = jnp.zeros((ROWS, LANES), jnp.float32)
                return 0

            lax.fori_loop(0, 4 + GROUP_STEPS, body, 0)

        return run

    pl.when(jnp.logical_not(has_right))(blank(0))
    pl.when(jnp.logical_not(has_left))(blank(1))
    for wait in wait_lanes:
        wait()

    def take_beside(r):
        rows, there = pl.ds(r, 8), pl.ds(pl.multiple_of(r + TOP, 8), 8)
        for f in range(4 + GROUP_STEPS):
            both = jnp.where(lane < HALF, beside[0, f, rows, :], beside[1, f, rows, :])
            if f < 2 + GROUP_STEPS:
                field[f, WRAP, there, :] = both
            else:
                own[f - 2 - GROUP_STEPS, WRAP, rows, :] = both

    by_rows(take_beside)
    wait_start += shift_on(own.at[0], start.at[0], WRAP, 1, 3)
    wait_rows += rows_beside(WRAP, 1, 12)

    def ring(t):
        return lax.rem(t + ALL, ALL)

    def both_sides(ref, t):
        def at(rows):
            return jnp.where(lane < HALF, ref(ring(t + 1), rows), ref(ring(t - 1), rows))

        return at

    for f in range(2):
        for r in range(0, ROWS, 8):
            kc_box[f, 0, pl.ds(r, 8), :] = field[f, me, pl.ds(TOP + r, 8), :]
            beside_me = both_sides(lambda c, rows, f=f: field[f, c, rows, :], me)(pl.ds(TOP + r, 8))
            kc_box[f, 1, pl.ds(r, 8), :] = beside_me
            kc[f, 0, pl.ds(CTOP + r, 8), :] = kc_box[f, 0, pl.ds(r, 8), :]
            kc[f, 1, pl.ds(CTOP + r, 8), :] = beside_me
    two = pl.ds(0, 2)
    wait_kc = [
        remote(kc_box.at[two, two, pl.ds(0, CHALO)], kc.at[two, two, pl.ds(CEND, CHALO)], 14,
               (me, gx - 1, gy), has_up, has_down),
        remote(kc_box.at[two, two, pl.ds(ROWS - CHALO, CHALO)], kc.at[two, two, pl.ds(GUARD, CHALO)], 15,
               (me, gx + 1, gy), has_down, has_up),
    ]

    def inside_rows(r, top):
        row = gx * ROWS + r - top + lax.broadcasted_iota(jnp.int32, (8, LANES), 0)
        return jnp.logical_and(row >= 0, row < n_gx * ROWS)

    wide_inside = jnp.logical_or(
        jnp.logical_and(lane < HALF, has_right), jnp.logical_and(lane >= HALF, has_left)
    )

    def inside(c, r):
        rows = inside_rows(r, TOP)
        return jnp.logical_and(rows, wide_inside) if c == WRAP else rows

    def put(c, rows, inverse, size, sides):
        for d, side in enumerate(sides):
            edges[d, c, rows, :] = inverse * side
        scale[c, rows, :] = inverse * size
        for n in range(GROUP_STEPS):
            loads[n, c, rows, :] = inverse * field[2 + n, c, rows, :]

    def fine_coefficients(lo, hi):
        def body(i, _):
            r = pl.multiple_of(i * 8, 8)
            coefficients(field.at[0], field.at[1], 1, inside, [r], ALL, put)
            return 0

        lax.fori_loop(lo // 8, hi // 8, body, 0)

    fine_coefficients(TOP + 8, END - 8)
    for wait in wait_rows:
        wait()
    fine_coefficients(GUARD, TOP + 8)
    fine_coefficients(END - 8, END + HALO)

    def relax(state, finish):
        def step(rows_of, n):
            args = (edges, held)
            whole = list(range(GUARD, END + HALO, 8)) if rows_of == 2 else list(range(GUARD + 8, END + HALO - 8, 8))
            sweep(*args, scale, loads.at[n], state, None, work, 1.0, whole, ALL)
            sweep(*args, None, None, work, state, state, weights[1], whole, ALL)
            sweep(*args, None, None, state, work, work, weights[2], whole, ALL)
            return whole

        def outer(n, _):
            whole = step(2, n)
            sweep(edges, held, None, None, work, state, state, weights[3], whole, ALL)
            return 0

        lax.fori_loop(0, 2, outer, 0)

        def inner(n, _):
            whole = step(1, n)
            sweep(edges, held, None, None, work, state, state, weights[3], whole, ALL)
            return 0

        lax.fori_loop(2, GROUP_STEPS, inner, 0)

        def copy_out(r):
            there = pl.ds(pl.multiple_of(r + TOP, 8), 8)
            for c in range(ALL):
                finish(c, r, state[c, there, :])

        by_rows(copy_out)

    for wait in wait_start:
        wait()

    def finish_relaxed(c, r, new):
        relaxed[c, pl.ds(r, 8), :] = new

    relax(start.at[0], finish_relaxed)

    def hand_over(r):
        last = me == n_tm - 1
        for c in range(ALL):
            rows = pl.ds(r, 8)
            own[2, c, rows, :] = jnp.where(last, own[1, c, rows, :], relaxed[c, rows, :])

    by_rows(hand_over)
    wait_second = shift_on(own.at[2], start.at[1], 0, ALL, 16)

    for wait in wait_kc:
        wait()

    chain_inside = jnp.logical_or(
        jnp.logical_and(lane < HALF, jnp.logical_or(me < n_tm - 1, has_right)),
        jnp.logical_and(lane >= HALF, jnp.logical_or(me > 0, has_left)),
    )

    def inside_chain(c, r):
        rows = inside_rows(r, CTOP)
        return jnp.logical_and(rows, chain_inside) if c else rows

    def put_chain(c, rows, inverse, size, sides):
        for d, side in enumerate(sides):
            cedges[d, c, rows, :] = inverse * side
        cscale[c, rows, :] = inverse * size

    def chain_coefficients(i, _):
        r = pl.multiple_of(GUARD + i * 32, 8)
        rows_of = [pl.multiple_of(r + 8 * u, 8) for u in range(4)]
        coefficients(kc.at[0], kc.at[1], GROUP_STEPS, inside_chain, rows_of, 2, put_chain)
        return 0

    lax.fori_loop(0, (ROWS + 2 * CHALO) // 32, chain_coefficients, 0)

    for wait in wait_second:
        wait()

    def finish_residual(c, r, new):
        rows = pl.ds(r, 8)
        left_over = new - relaxed[c, rows, :]
        residual[c, rows, :] = left_over
        if c < TILES:
            result[0, rows, columns(c)] = left_over

    relax(start.at[1], finish_residual)
    put_residual = pltpu.make_async_copy(result.at[0], residual_hbm.at[0], out_sem.at[0])
    put_residual.start()

    def fill_box(r):
        rows = pl.ds(r, 8)
        for t in range(TILES):
            box[t, 0, rows, :] = residual[t, rows, :]
            box[t, 1, rows, :] = jnp.where(
                lane < HALF, residual[(t + 1) % ALL, rows, :], residual[(t - 1) % ALL, rows, :]
            )

    by_rows(fill_box)

    def to_chain(src, dst, kind, d, device):
        return pltpu.make_async_remote_copy(
            src_ref=src,
            dst_ref=dst,
            send_sem=a2a_send.at[kind, d],
            recv_sem=a2a_recv.at[kind, me],
            device_id=device,
            device_id_type=MESH,
        )

    def centre(d):
        t = lax.rem(me + d, n_tm)
        return to_chain(box.at[t], arrived.at[me, two, pl.ds(CTOP, ROWS)], 0, d, (t, gx, gy))

    def upward(d, tall):
        t = lax.rem(me + d, n_tm)
        return to_chain(
            box.at[t, two, pl.ds(0, tall)], arrived.at[me, two, pl.ds(CEND, tall)], 1, d, (t, gx - 1, gy)
        )

    def downward(d, tall):
        t = lax.rem(me + d, n_tm)
        return to_chain(
            box.at[t, two, pl.ds(ROWS - tall, tall)],
            arrived.at[me, two, pl.ds(CTOP - tall, tall)],
            2, d, (t, gx + 1, gy),
        )

    here = pltpu.make_async_copy(box.at[me], arrived.at[me, two, pl.ds(CTOP, ROWS)], local_sem.at[0])
    here.start()

    def each(lo, act):
        def run(d, _):
            act(d)
            return 0

        lax.fori_loop(lo, n_tm, run, 0)

    each(1, lambda d: centre(d).start())
    talls = sorted({strip(k) for k in range(n_tm)} - {0})
    for tall in talls:
        ks = [k for k in range(n_tm) if strip(k) == tall]
        mine = jnp.logical_and(me >= ks[0], me <= ks[-1])
        pl.when(jnp.logical_and(mine, has_up))(
            lambda tall=tall: each(0, lambda d: upward(d, tall).start())
        )
        pl.when(jnp.logical_and(mine, has_down))(
            lambda tall=tall: each(0, lambda d: downward(d, tall).start())
        )

    def incoming(dst, kind, k):
        return pltpu.make_async_remote_copy(
            src_ref=dst,
            dst_ref=dst,
            send_sem=a2a_send.at[kind, 0],
            recv_sem=a2a_recv.at[kind, k],
            device_id=(me, gx, gy),
            device_id_type=MESH,
        )

    here.wait()
    for k in range(n_tm):
        pl.when(me != k)(incoming(arrived.at[k, two, pl.ds(CTOP, ROWS)], 0, k).wait_recv)
        if strip(k):
            pl.when(has_down)(incoming(arrived.at[k, two, pl.ds(CEND, strip(k))], 1, k).wait_recv)
            pl.when(has_up)(
                incoming(arrived.at[k, two, pl.ds(CTOP - strip(k), strip(k))], 2, k).wait_recv
            )

    def give_back(k):
        return pltpu.make_async_remote_copy(
            src_ref=out_box.at[k],
            dst_ref=error.at[me],
            send_sem=back_send.at[k],
            recv_sem=back_recv.at[me],
            device_id=(k, gx, gy),
            device_id_type=MESH,
        )

    def keep(k):
        return pltpu.make_async_copy(out_box.at[k], error.at[me], local_sem.at[1])

    def hand_back(k):
        for r in range(0, ROWS, 8):
            out_box[k, pl.ds(r, 8), :] = chain[0, pl.ds(CTOP + r, 8), :]
        pl.when(me == k)(lambda: keep(k).start())
        pl.when(me != k)(lambda: give_back(k).start())

    chain[...] = arrived[0]
    hand_back(0)

    def link(k, _):
        rows_of = list(range(GUARD, CEND + CHALO, 8))
        sweep(cedges, cheld, cscale, None, chain, None, chain_work, 1.0, rows_of, 2)
        sweep(cedges, cheld, None, None, chain_work, chain, chain, weights[1], rows_of, 2)
        sweep(cedges, cheld, None, None, chain, chain_work, chain_work, weights[2], rows_of, 2)

        def add(c, r, new):
            chain[c, pl.ds(r, 8), :] = new + arrived[k, c, pl.ds(r, 8), :]

        sweep(cedges, cheld, None, None, chain_work, chain, None, weights[3], rows_of, 2, add)
        hand_back(k)
        return 0

    lax.fori_loop(1, n_tm, link, 0)

    for t in range(n_tm):
        pl.when(me == t)(lambda t=t: keep(t).wait())
        pl.when(me != t)(
            pltpu.make_async_remote_copy(
                src_ref=error.at[t],
                dst_ref=error.at[t],
                send_sem=back_send.at[t],
                recv_sem=back_recv.at[t],
                device_id=(me, gx, gy),
                device_id_type=MESH,
            ).wait_recv
        )

    def correct(r):
        rows = pl.ds(r, 8)
        for c in range(TILES):
            result[1, rows, columns(c)] = relaxed[c, rows, :] + error[c, rows, :]

    by_rows(correct)
    put_corrected = pltpu.make_async_copy(result.at[1], corrected_hbm.at[0], out_sem.at[1])
    put_corrected.start()

    for copy, sends in started:
        if sends is None:
            copy.wait_send()
        else:
            pl.when(sends)(copy.wait_send)
    each(1, lambda d: centre(d).wait_send())
    for tall in talls:
        ks = [k for k in range(n_tm) if strip(k) == tall]
        mine = jnp.logical_and(me >= ks[0], me <= ks[-1])
        pl.when(jnp.logical_and(mine, has_up))(
            lambda tall=tall: each(0, lambda d: upward(d, tall).wait_send())
        )
        pl.when(jnp.logical_and(mine, has_down))(
            lambda tall=tall: each(0, lambda d: downward(d, tall).wait_send())
        )
    for k in range(n_tm):
        pl.when(me != k)(lambda k=k: give_back(k).wait_send())
    put_residual.wait()
    put_corrected.wait()


def shards(sizes, *args):
    f32 = jnp.float32
    vmem = lambda *shape: pltpu.VMEM(shape, f32)
    wide = (ALL, TALL, LANES)
    slim = (2, CTALL, LANES)
    flat = (ALL, ROWS, LANES)
    block = (ROWS, TILES * LANES)
    anywhere = pl.BlockSpec(memory_space=pl.ANY)
    scalars = pl.BlockSpec(memory_space=pltpu.SMEM)
    dma = pltpu.SemaphoreType.DMA
    out = jax.ShapeDtypeStruct((1,) + block, f32)
    return pl.pallas_call(
        functools.partial(kernel, sizes),
        out_shape=(out, out),
        in_specs=[anywhere, anywhere, anywhere, scalars, anywhere, anywhere, anywhere, scalars],
        out_specs=(anywhere, anywhere),
        scratch_shapes=[
            vmem(4, *block),
            pltpu.VMEM((1 + GROUP_STEPS,) + block, jnp.int32),
            vmem(2 + GROUP_STEPS, *wide),
            vmem(3, *flat),
            vmem(2, 4 + GROUP_STEPS, ROWS, LANES),
            vmem(2, *wide),
            vmem(*wide),
            vmem(*wide),
            vmem(4, *wide),
            vmem(*wide),
            vmem(GROUP_STEPS, *wide),
            vmem(*flat),
            vmem(*flat),
            vmem(TILES, 2, ROWS, LANES),
            vmem(TILES, *slim),
            vmem(2, *slim),
            vmem(2, 2, ROWS, LANES),
            vmem(4, *slim),
            vmem(*slim),
            vmem(*slim),
            vmem(*slim),
            vmem(*slim),
            vmem(TILES, ROWS, LANES),
            vmem(TILES, ROWS, LANES),
            vmem(2, *block),
            dma((6,)),
            dma((2,)),
            dma((2,)),
            dma((19,)),
            dma((19,)),
            dma((3, TILES)),
            dma((3, TILES)),
            dma((TILES,)),
            dma((TILES,)),
        ],
        compiler_params=pltpu.CompilerParams(
            collective_id=0, has_side_effects=True, vmem_limit_bytes=48 * 2**20
        ),
    )(*args)


def solution(mesh):
    placed = (
        P("gx", "gy"),
        P("tm", "gx", "gy"),
        P("gx", "gy"),
        P(),
        P("gx", "gy"),
        P("gx", "gy"),
        P("tm", "gx", "gy"),
        P(),
    )
    sizes = (mesh.shape["tm"], mesh.shape["gx"], mesh.shape["gy"])
    return jax.shard_map(
        functools.partial(shards, sizes),
        mesh=mesh,
        in_specs=placed,
        out_specs=(P("tm", "gx", "gy"), P("tm", "gx", "gy")),
        check_vma=False,
    )
```

time: 1240 us -> 61.5 us (0.05); the launches traced: 1210 us -> 60.3 us
  starting transfers between devices: 922 us -> 0 us
  waiting for transfers between devices: 237 us -> 0 us
  Pallas kernels: 0 us -> 50.9 us
  other arithmetic: 44.9 us -> 0 us
    ppermute x270 -> x0, starting transfers between devices: 922 us -> none  [the longest x130 438 us: with_halo(): lax.ppermute(lax.slice_in_dim(block, block.shape[dim] - width, None, axis...]
    ppermute x270 -> x0, waiting for transfers between devices: 237 us -> none  [the longest x130 151 us: with_halo(): lax.ppermute(lax.slice_in_dim(block, 0, width, axis=dim), axis, backward)]
    pallas_call x0 -> x1, Pallas kernels: none -> 50.9 us  [shards(): pl.pallas_call(functools.partial(kernel, sizes), out_shape=(out, out), in...]
    add x63 -> x0, other arithmetic: 32.1 us -> none  [the longest x55 29.6 us: chebyshev(): newest = weight * (jacobi - previous) + previous]
  transfers between devices with their start and end apart: 270 -> 0, of which waited for: 139 -> 0; matrix products, arithmetic and copies ran while one was open for 0% -> 0% of each run, Pallas kernels for 0% -> 0%
where the time goes in v1:
time: 61.5 us; the launch traced here: 60.3 us
  Pallas kernels  50.9 us (83%)
  local copies, waits for them, and re-layouts  8.68 us (14%)
  between operations  0.66 us (1%)
    pallas_call x1, Pallas kernels, shards(): pl.pallas_call(functools.partial(kernel, sizes), out_shape=(out, out), in...  50.9 us
    unnamed x18, local copies, waits for them, and re-layouts  8.68 us

profile of v1, /device:TPU:77, one launch (start us, length us, event | category | flops | bytes accessed | tf_op | source)
XLA Modules:
  0.0 60.3 jit_solution(3925479717105621371)
XLA Ops:
  0.6 0.0 copy-start
  0.6 1.2 %copy-done = s32[4,64,1024]{2,1,0:T(8,128)S(1)} copy-done((s32[4,64,1024]{2,1,0:T(8,128)S(1)}, s32[4,64,1024]{2,1,0:T(8,128)}, u32[]{:S(2)}) %copy-start) | copy-done | bytes 1048600
  1.9 0.0 copy-start.1
  1.9 0.9 %copy-done.1 = f32[64,1024]{1,0:T(8,128)S(1)} copy-done((f32[64,1024]{1,0:T(8,128)S(1)}, f32[64,1024]{1,0:T(8,128)}, u32[]{:S(2)}) %copy-start.1) | copy-done | bytes 262168
  2.8 0.0 copy-start.2
  2.8 0.9 %copy-done.2 = f32[1,64,1024]{2,1,0:T(8,128)S(1)} copy-done((f32[1,64,1024]{2,1,0:T(8,128)S(1)}, f32[1,64,1024]{2,1,0:T(8,128)}, u32[]{:S(2)}) %copy-start.2) | copy-done | bytes 262168
  3.8 0.0 copy-start.3
  3.8 0.9 %copy-done.3 = s32[64,1024]{1,0:T(8,128)S(1)} copy-done((s32[64,1024]{1,0:T(8,128)S(1)}, s32[64,1024]{1,0:T(8,128)}, u32[]{:S(2)}) %copy-start.3) | copy-done | bytes 262168
  4.7 0.0 copy-start.4
  4.7 0.9 %copy-done.4 = f32[64,1024]{1,0:T(8,128)S(1)} copy-done((f32[64,1024]{1,0:T(8,128)S(1)}, f32[64,1024]{1,0:T(8,128)}, u32[]{:S(2)}) %copy-start.4) | copy-done | bytes 262168
  5.7 0.0 copy-start.5
  5.7 0.9 %copy-done.5 = f32[64,1024]{1,0:T(8,128)S(1)} copy-done((f32[64,1024]{1,0:T(8,128)S(1)}, f32[64,1024]{1,0:T(8,128)}, u32[]{:S(2)}) %copy-start.5) | copy-done | bytes 262168
  6.6 0.0 copy-start.6
  6.6 0.7 %copy-done.6 = f32[8]{0:T(128)S(1)} copy-done((f32[8]{0:T(128)S(1)}, f32[8]{0:T(128)}, u32[]{:S(2)}) %copy-start.6) | copy-done | bytes 56
  7.3 0.0 copy-start.7
  7.3 0.7 %copy-done.7 = f32[4]{0:T(128)S(1)} copy-done((f32[4]{0:T(128)S(1)}, f32[4]{0:T(128)}, u32[]{:S(2)}) %copy-start.7) | copy-done | bytes 40
  7.9 50.9 %shard_map.95 = (f32[1,64,1024]{2,1,0:T(8,128)S(1)}, f32[1,64,1024]{2,1,0:T(8,128)S(1)}) custom-call(f32[64,1024]{1,0:T(8,128)S(1)} %copy-done.1, f32[1,64,1024]{2,1,0:T(8,128)S(1)} %copy-done.2, s32[64,1024]{1,0:T(8,128)S(1)} %copy-done.3, f32[8]{0:T(128)S(1)} %copy-done.6, f32[64,1024]{1,0:T(8,128)S(1)} %copy-done.4, f32[64,1024]{1,0:T(8,128)S(1)} %copy-done.5, ...), custom_call_target="tpu_custom_call" | custom-call | tf_op jit(solution)/shard_map/pallas_call | solution.py:637
  58.9 0.7 %copy.12 = f32[1,64,1024]{2,1,0:T(8,128)} copy(f32[1,64,1024]{2,1,0:T(8,128)S(1)} %get-tuple-element.4) | data formatting | bytes 524288
  59.6 0.7 %copy.13 = f32[1,64,1024]{2,1,0:T(8,128)} copy(f32[1,64,1024]{2,1,0:T(8,128)S(1)} %get-tuple-element.5) | data formatting | bytes 524288
Async XLA Ops:
  0.6 1.2 %copy-start = (s32[4,64,1024]{2,1,0:T(8,128)S(1)}, s32[4,64,1024]{2,1,0:T(8,128)}, u32[]{:S(2)}) copy-start(s32[4,64,1024]{2,1,0:T(8,128)} %tap_hbm.1) | copy-start | bytes 3145732
  1.9 0.9 %copy-start.1 = (f32[64,1024]{1,0:T(8,128)S(1)}, f32[64,1024]{1,0:T(8,128)}, u32[]{:S(2)}) copy-start(f32[64,1024]{1,0:T(8,128)} %initial_hbm.1) | copy-start | bytes 786436
  2.8 0.9 %copy-start.2 = (f32[1,64,1024]{2,1,0:T(8,128)S(1)}, f32[1,64,1024]{2,1,0:T(8,128)}, u32[]{:S(2)}) copy-start(f32[1,64,1024]{2,1,0:T(8,128)} %guess_hbm.1) | copy-start | bytes 786436
  3.8 0.9 %copy-start.3 = (s32[64,1024]{1,0:T(8,128)S(1)}, s32[64,1024]{1,0:T(8,128)}, u32[]{:S(2)}) copy-start(s32[64,1024]{1,0:T(8,128)} %class_hbm.1) | copy-start | bytes 786436
  4.7 0.9 %copy-start.4 = (f32[64,1024]{1,0:T(8,128)S(1)}, f32[64,1024]{1,0:T(8,128)}, u32[]{:S(2)}) copy-start(f32[64,1024]{1,0:T(8,128)} %cap_hbm.1) | copy-start | bytes 786436
  5.7 0.9 %copy-start.5 = (f32[64,1024]{1,0:T(8,128)S(1)}, f32[64,1024]{1,0:T(8,128)}, u32[]{:S(2)}) copy-start(f32[64,1024]{1,0:T(8,128)} %base_hbm.1) | copy-start | bytes 786436
  6.6 0.7 %copy-start.6 = (f32[8]{0:T(128)S(1)}, f32[8]{0:T(128)}, u32[]{:S(2)}) copy-start(f32[8]{0:T(128)} %conductance.1) | copy-start | bytes 100
  7.3 0.7 %copy-start.7 = (f32[4]{0:T(128)S(1)}, f32[4]{0:T(128)}, u32[]{:S(2)}) copy-start(f32[4]{0:T(128)} %levels.1) | copy-start | bytes 52

commit v2 on v0

v2 whole, which is shorter than its diff:
```python
import functools

import jax
import jax.numpy as jnp
from jax import lax
from jax.experimental import pallas as pl
from jax.experimental.pallas import tpu as pltpu
from jax.sharding import PartitionSpec as P

GROUP_STEPS = 4
SWEEPS = 4
NCLS = 8
NLEV = 4
RHO = 0.9

LANES = 128
HALF = 64
ROWS = 64
TILES = 8
WRAP = TILES
ALL = TILES + 1
PART = TILES // 2
RING = PART + 1
HALO = 16
GUARD = 8
TOP = GUARD + HALO
END = TOP + ROWS
TALL = END + HALO + GUARD
NEAR = 8

CHALO = 24
CTOP = GUARD + CHALO
CEND = CTOP + ROWS
CTALL = CEND + CHALO + GUARD

KAPPA, CAP, LOAD = 0, 1, 2
FIELDS = LOAD + GROUP_STEPS
PAIRS = FIELDS // 2

MESH = pl.DeviceIdType.MESH
COPIES = 64


def cheb_weights(sweep_total):
    weights = [1.0]
    while len(weights) < sweep_total:
        if len(weights) == 1:
            weights.append(1.0 / (1.0 - RHO * RHO / 2.0))
        else:
            weights.append(1.0 / (1.0 - RHO * RHO * weights[-1] / 4.0))
    return weights


def strip(j):
    return 2 * SWEEPS * (TILES // 2 - 1 - j)


def lane_no():
    return lax.broadcasted_iota(jnp.int32, (8, LANES), 1)


def beside_lanes(tiles, c):
    lane = lane_no()
    n = len(tiles)
    left = pltpu.roll(jnp.where(lane == LANES - 1, tiles[c - 1], tiles[c]), 1, 1)
    right = pltpu.roll(jnp.where(lane == 0, tiles[(c + 1) % n], tiles[c]), LANES - 1, 1)
    return left, right


def sweep(edges, held, base_of, cur, prev, dst, weight, rows_of, tiles, after=None):
    first = base_of is not None
    for r in rows_of:
        rows = pl.ds(r, 8)
        here = [cur[c, rows, :] for c in range(tiles)]
        for c in range(tiles):
            left, right = beside_lanes(here, c)
            up = cur[c, pl.ds(r - 1, 8), :]
            down = cur[c, pl.ds(r + 1, 8), :]
            if first:
                base = base_of(c, rows, here[c])
                held[c, rows, :] = base
            else:
                base = held[c, rows, :]
            new = base + (
                (edges[0, c, rows, :] * up + edges[1, c, rows, :] * down)
                + (edges[2, c, rows, :] * left + edges[3, c, rows, :] * right)
            )
            if not first:
                before = prev[c, rows, :]
                new = weight * (new - before) + before
            if after is None:
                dst[c, rows, :] = new
            else:
                after(c, r, new)


def solve(edges, held, base_of, state, work, rows_of, tiles, after=None):
    w = cheb_weights(SWEEPS)
    sweep(edges, held, base_of, state, None, work, w[0], rows_of, tiles)
    sweep(edges, held, None, work, state, state, w[1], rows_of, tiles)
    sweep(edges, held, None, state, work, work, w[2], rows_of, tiles)
    sweep(edges, held, None, work, state, state, w[3], rows_of, tiles, after)


def coefficients(kappa, cap, divide, inside, r, tiles, put):
    rows = pl.ds(r, 8)
    here = [kappa(c, rows) for c in range(tiles)]
    for c in range(tiles):
        left, right = beside_lanes(here, c)
        west = 0.5 * (kappa(c, pl.ds(r - 1, 8)) + here[c])
        east = 0.5 * (here[c] + kappa(c, pl.ds(r + 1, 8)))
        south = 0.5 * (left + here[c])
        north = 0.5 * (here[c] + right)
        size = cap(c, rows) * (1.0 / divide)
        diag = size + west + east + south + north
        ok = inside(c, r)
        inverse = jnp.where(ok, 1.0 / jnp.where(ok, diag, 1.0), 0.0)
        put(c, rows, inverse, size, (west, east, south, north))


def kernel(
    sizes,
    initial_hbm, guess_hbm, class_hbm, conductance_hbm, cap_hbm, base_hbm, tap_hbm, levels_hbm,
    relaxed_out, error_out, again_out,
    raw, raw_index, field, guess, initial, lane_box, beside, guess_beside, initial_beside, start, work, held, edges, scale, inv,
    relaxed, hand, residual, comb, partner, gedges, gscale, box, arrived, kc, kc_box,
    cedges, cscale, cheld, chain, chain_work, out_box, error, conductance, levels,
    in_sem, local_sem, send, recv, a2a_send, a2a_recv, back_send, back_recv,
):
    n_tm, n_gx, n_gy = sizes
    me = lax.axis_index("tm")
    gx = lax.axis_index("gx")
    gy = lax.axis_index("gy")
    lane = lane_no()
    low, high = lane < HALF, lane >= HALF
    has_up, has_down = gx > 0, gx < n_gx - 1
    has_left, has_right = gy > 0, gy < n_gy - 1
    later = lax.rem(me + 1, n_tm)
    odd = lax.rem(me, 2)
    is_even, is_odd = odd == 0, odd == 1
    pair, quarter = lax.div(me, 2), lax.div(me, PART)

    loads_in = [
        pltpu.make_async_copy(guess_hbm.at[0], raw.at[0], in_sem.at[0]),
        pltpu.make_async_copy(class_hbm, raw_index.at[0], in_sem.at[1]),
        pltpu.make_async_copy(cap_hbm, raw.at[1], in_sem.at[2]),
        pltpu.make_async_copy(base_hbm, raw.at[2], in_sem.at[3]),
        pltpu.make_async_copy(tap_hbm, raw_index.at[pl.ds(1, GROUP_STEPS)], in_sem.at[4]),
        pltpu.make_async_copy(initial_hbm, raw.at[3], in_sem.at[5]),
        pltpu.make_async_copy(conductance_hbm, conductance, in_sem.at[6]),
        pltpu.make_async_copy(levels_hbm, levels, in_sem.at[7]),
    ]
    for copy in loads_in:
        copy.start()

    def clear(ref, lead, tall, top, end):
        zero = jnp.zeros((8, LANES), jnp.float32)
        for r in list(range(0, top, 8)) + list(range(end, tall, 8)):
            for c in range(ref.shape[len(lead)]):
                ref[lead + (c, pl.ds(r, 8), slice(None))] = zero

    def many(lo, hi, act):
        def run(i, _):
            act(i)
            return 0

        lax.fori_loop(lo, hi, run, 0)

    def rows_from(lo, hi, body):
        many(lo // 8, hi // 8, lambda i: body(pl.multiple_of(i * 8, 8)))

    def by_rows(body):
        rows_from(0, ROWS, body)

    def columns(c):
        return slice(c * LANES, (c + 1) * LANES)

    many(0, FIELDS, lambda f: clear(field, (f,), TALL, TOP, END))

    def clear_parts(h):
        clear(start, (0, h), TALL, TOP, END)
        clear(start, (1, h), TALL, TOP, END)
        clear(kc, (h,), CTALL, CTOP, CEND)
        clear(beside, (h,), TALL, TOP, END)

    many(0, 2, clear_parts)
    clear(guess_beside, (), TALL, TOP, END)
    clear(comb, (), TALL, TOP, END)
    clear(work, (), TALL, TOP, END)
    clear(chain_work, (), CTALL, CTOP, CEND)
    many(0, n_tm // 2, lambda j: clear(arrived, (j,), CTALL, CTOP, CEND))

    def blank(side):
        def run():
            def fill(r):
                rows = pl.ds(pl.multiple_of(r + TOP, 8), 8)
                zero = jnp.zeros((8, LANES), jnp.float32)
                guess_beside[side, rows, :] = zero
                initial_beside[side, pl.ds(r, 8), :] = zero
                for q in range(PAIRS):
                    beside[side, q, rows, :] = zero

            by_rows(fill)

        return run

    pl.when(jnp.logical_not(has_right))(blank(0))
    pl.when(jnp.logical_not(has_left))(blank(1))

    barrier = pltpu.get_barrier_semaphore()

    def greet(t, x, y):
        pl.semaphore_signal(barrier, inc=1, device_id=(t, x, y), device_id_type=MESH)

    def greet_column(t, y):
        greet(t, gx, y)
        pl.when(has_up)(lambda: greet(t, gx - 1, y))
        pl.when(has_down)(lambda: greet(t, gx + 1, y))

    for d in range(n_tm):
        t = lax.rem(me + d, n_tm)
        if d:
            greet(t, gx, gy)
        pl.when(has_up)(lambda t=t: greet(t, gx - 1, gy))
        pl.when(has_down)(lambda t=t: greet(t, gx + 1, gy))
    for t in (me, lax.rem(me + n_tm - 1, n_tm)):
        pl.when(has_left)(lambda t=t: greet_column(t, gy - 1))
        pl.when(has_right)(lambda t=t: greet_column(t, gy + 1))
    one = lambda flag: flag.astype(jnp.int32)
    tall_friends = 1 + one(has_up) + one(has_down)
    friends = (n_tm + 2 * (one(has_left) + one(has_right))) * tall_friends - 1

    for copy in loads_in:
        copy.wait()

    def take_fields(r):
        rows, there = pl.ds(r, 8), pl.ds(pl.multiple_of(r + TOP, 8), 8)
        ends, known = {}, []
        for c in range(TILES):
            kind = raw_index[0, rows, columns(c)]
            kappa = jnp.full((8, LANES), conductance[0], jnp.float32)
            for j in range(1, NCLS):
                kappa = jnp.where(kind == j, conductance[j], kappa)
            cap = raw[1, rows, columns(c)]
            field[KAPPA, c, there, :] = kappa
            field[CAP, c, there, :] = cap
            peak = raw[2, rows, columns(c)]
            load = []
            for n in range(GROUP_STEPS):
                tap = raw_index[1 + n, rows, columns(c)]
                level = jnp.full((8, LANES), levels[0], jnp.float32)
                for j in range(1, NLEV):
                    level = jnp.where(tap == j, levels[j], level)
                load.append(peak * level)
                field[LOAD + n, c, there, :] = load[n]
            initial[c // PART, c % PART, rows, :] = raw[3, rows, columns(c)]
            known.append(raw[0, rows, columns(c)])
            guess[c // PART, c % PART, rows, :] = known[c]
            ends[c] = [kappa, cap] + load
        guess[0, PART, rows, :] = jnp.where(low, known[PART], known[PART - 1])
        first, last_tile = ends[0], ends[TILES - 1]
        for q in range(PAIRS):
            a, b = 2 * q, 2 * q + 1
            lane_box[0, q, rows, :] = jnp.where(low, first[a], pltpu.roll(first[b], HALF, 1))
            lane_box[1, q, rows, :] = jnp.where(low, pltpu.roll(last_tile[b], HALF, 1), last_tile[a])

    by_rows(take_fields)

    pl.semaphore_wait(barrier, friends)

    made = []
    both = jnp.logical_and
    last = me == n_tm - 1

    def remote(src, dst, device, sends=None, receives=None):
        no = len(made)
        copy = pltpu.make_async_remote_copy(
            src_ref=src,
            dst_ref=dst,
            send_sem=send.at[no],
            recv_sem=recv.at[no],
            device_id=device,
            device_id_type=MESH,
        )
        made.append((copy, sends, receives))
        return no

    def act_on(nos, what, which):
        for no in nos:
            flag = made[no][which]
            if flag is None:
                getattr(made[no][0], what)()
            else:
                pl.when(flag)(getattr(made[no][0], what))

    def begin(nos):
        act_on(nos, "start", 1)
        return nos

    def wait_for(nos):
        act_on(nos, "wait_recv", 2)

    centre_rows = pl.ds(TOP, ROWS)

    def up_and_down(source, target, rows, top, t, source_top=0):
        if source_top:
            lo, hi = pl.ds(source_top, rows), pl.ds(source_top + ROWS - rows, rows)
        else:
            lo, hi = pl.ds(0, rows), pl.ds(ROWS - rows, rows)
        return [
            remote(source(lo), target(pl.ds(top + ROWS, rows)), (t, gx - 1, gy), has_up, has_down),
            remote(source(hi), target(pl.ds(top - rows, rows)), (t, gx + 1, gy), has_down, has_up),
        ]

    def to_corners(source, target, rows, t):
        nos = []
        for side, y, flag, back in ((0, gy - 1, has_left, has_right), (1, gy + 1, has_right, has_left)):
            nos.append(
                remote(source(side, pl.ds(0, rows)), target(side, pl.ds(END, rows)),
                       (t, gx - 1, y), both(flag, has_up), both(back, has_down))
            )
            nos.append(
                remote(source(side, pl.ds(ROWS - rows, rows)), target(side, pl.ds(TOP - rows, rows)),
                       (t, gx + 1, y), both(flag, has_down), both(back, has_up))
            )
        return nos

    def left_and_right(source, target, t, where=None, there=None):
        nos = []
        for side, y, flag, back in ((0, gy - 1, has_left, has_right), (1, gy + 1, has_right, has_left)):
            if where is not None:
                flag, back = both(flag, where), both(back, there)
            nos.append(remote(source(side), target(side), (t, gx, y), flag, back))
        return nos

    def shift_on(source, target, lo, count):
        part = pl.ds(lo, count)
        centre = remote(source.at[part], target.at[part, centre_rows], (later, gx, gy))
        rest = up_and_down(
            lambda rows: source.at[part, rows], lambda rows: target.at[part, rows], HALO, TOP, later
        )
        return [centre] + rest

    def rows_beside(f, count, lo, tiles, rows):
        fs, part = pl.ds(f, count), pl.ds(lo, tiles)
        at = lambda rows: field.at[fs, part, rows]
        return up_and_down(at, at, rows, TOP, me, TOP)

    def end_tile(side, rows):
        return guess.at[side, 0 if side == 0 else PART - 1, rows]

    every = pl.ds(0, ROWS)
    early, rest = pl.ds(0, 2), pl.ds(2, 1)
    send_lanes = begin(
        left_and_right(
            lambda side: lane_box.at[side, early], lambda side: beside.at[side, early, centre_rows], me
        )
    )
    send_guess_lanes = begin(
        left_and_right(
            lambda side: end_tile(side, every), lambda side: guess_beside.at[side, centre_rows], later
        )
    )
    send_corners = begin(
        to_corners(
            lambda side, rows: lane_box.at[side, early, rows],
            lambda side, rows: beside.at[side, early, rows], HALO, me,
        )
        + to_corners(end_tile, lambda side, rows: guess_beside.at[side, rows], HALO, later)
    )
    send_first = begin(
        rows_beside(KAPPA, 3, 0, RING, HALO) + shift_on(guess.at[0], start.at[0, 0], 0, RING)
    )
    send_load = begin(rows_beside(LOAD + 1, 1, 0, RING, HALO))
    send_second = begin(
        rows_beside(KAPPA, 4, RING, TILES - RING, HALO) + shift_on(guess.at[1], start.at[0, 1], 0, PART)
    )
    send_late = begin(
        rows_beside(LOAD + 2, 2, 0, TILES, NEAR)
        + left_and_right(
            lambda side: lane_box.at[side, rest], lambda side: beside.at[side, rest, centre_rows], me
        )
        + to_corners(
            lambda side, rows: lane_box.at[side, rest, rows],
            lambda side, rows: beside.at[side, rest, rows], NEAR, me,
        )
        + left_and_right(
            lambda side: initial.at[side, 0 if side == 0 else PART - 1],
            lambda side: initial_beside.at[side], me, last, last,
        )
    )
    two = pl.ds(0, 2)
    send_kc = up_and_down(
        lambda rows: kc_box.at[two, two, rows], lambda rows: kc.at[two, two, rows], CHALO, CTOP, me
    )
    send_relaxed = [shift_on(hand.at[h], start.at[1, h], 0, RING) for h in range(2)]
    near, far = pl.ds(0, NEAR), pl.ds(ROWS - NEAR, NEAR)
    above, below = pl.ds(TOP - NEAR, NEAR), pl.ds(END, NEAR)
    send_residual = [
        [
            remote(residual.at[0], partner, (me - 1, gx, gy), is_odd, is_even),
            remote(residual.at[0, :, near], comb.at[:, below], (me, gx - 1, gy),
                   both(is_even, has_up), both(is_even, has_down)),
            remote(residual.at[0, :, far], comb.at[:, above], (me, gx + 1, gy),
                   both(is_even, has_down), both(is_even, has_up)),
        ],
        [
            remote(residual.at[1], comb.at[:, centre_rows], (me + 1, gx, gy), is_even, is_odd),
            remote(residual.at[1, :, near], comb.at[:, below], (me + 1, gx - 1, gy),
                   both(is_even, has_up), both(is_odd, has_down)),
            remote(residual.at[1, :, far], comb.at[:, above], (me + 1, gx + 1, gy),
                   both(is_even, has_down), both(is_odd, has_up)),
        ],
    ]

    def unpack(q, rows):
        right, left = beside[0, q, rows, :], beside[1, q, rows, :]
        return jnp.where(low, right, left), pltpu.roll(jnp.where(low, left, right), HALF, 1)

    def take_beside(r):
        rows = pl.ds(r, 8)
        field[KAPPA, WRAP, rows, :], field[CAP, WRAP, rows, :] = unpack(0, rows)
        field[LOAD, WRAP, rows, :], field[LOAD + 1, WRAP, rows, :] = unpack(1, rows)

    def take_beside_late(r):
        rows = pl.ds(r, 8)
        field[LOAD + 2, WRAP, rows, :], field[LOAD + 3, WRAP, rows, :] = unpack(2, rows)

    def close_guess(r):
        rows = pl.ds(r, 8)
        middle = start[0, 0, PART, rows, :]
        beyond = jnp.where(low, guess_beside[0, rows, :], guess_beside[1, rows, :])
        start[0, 0, PART, rows, :] = jnp.where(low, middle, beyond)
        start[0, 1, PART, rows, :] = jnp.where(low, beyond, middle)

    def close_initial(r):
        rows = pl.ds(r, 8)
        beyond = jnp.where(low, initial_beside[0, rows, :], initial_beside[1, rows, :])
        initial[0, PART, rows, :] = jnp.where(low, initial[1, 0, rows, :], beyond)
        initial[1, PART, rows, :] = jnp.where(low, beyond, initial[0, PART - 1, rows, :])

    def tile(f, h):
        def at(c, rows):
            if c < PART:
                return field[f, PART * h + c, rows, :]
            return jnp.where(
                low, field[f, PART + PART * h, rows, :], field[f, WRAP - RING * h, rows, :]
            )

        return at

    def inside_rows(r, top):
        row = gx * ROWS + r - top + lax.broadcasted_iota(jnp.int32, (8, LANES), 0)
        return both(row >= 0, row < n_gx * ROWS)

    def inside_part(h):
        right, left = jnp.logical_or(h == 0, has_right), jnp.logical_or(h == 1, has_left)
        wrapped = jnp.logical_or(both(low, right), both(high, left))

        def inside(c, r):
            rows = inside_rows(r, TOP)
            return both(rows, wrapped) if c == PART else rows

        return inside

    def fine_coefficients(h, lo, hi):
        def put(c, rows, inverse, size, sides):
            for d, side in enumerate(sides):
                edges[h, d, c, rows, :] = inverse * side
            scale[h, c, rows, :] = inverse * size
            inv[h, c, rows, :] = inverse

        def body(r):
            coefficients(tile(KAPPA, h), tile(CAP, h), 1, inside_part(h), r, RING, put)

        rows_from(lo, hi, body)

    wait_for(send_lanes)
    rows_from(TOP, END, take_beside)
    many(0, 2, lambda h: fine_coefficients(h, TOP + 8, END - 8))

    def ring(t):
        return lax.rem(t + ALL, ALL)

    for f in range(2):
        for r in range(0, ROWS, 8):
            rows, there = pl.ds(r, 8), pl.ds(TOP + r, 8)
            own = field[f, me, there, :]
            wide = jnp.where(low, field[f, ring(me + 1), there, :], field[f, ring(me - 1), there, :])
            kc_box[f, 0, rows, :] = own
            kc_box[f, 1, rows, :] = wide
            kc[f, 0, pl.ds(CTOP + r, 8), :] = own
            kc[f, 1, pl.ds(CTOP + r, 8), :] = wide
    begin(send_kc)

    def relax(state, h, finish, second=None, third=None):
        def step(n, rows_of):
            def base_of(c, rows, value):
                return scale[h, c, rows, :] * value + inv[h, c, rows, :] * tile(LOAD + n, h)(c, rows)

            solve(edges.at[h], held, base_of, state, work, rows_of, RING)

        def outer(n):
            if second is not None:
                pl.when(both(h == 0, n == 1))(second)
            step(n, list(range(GUARD, END + HALO, 8)))

        many(0, 2, outer)
        if third is not None:
            pl.when(h == 0)(third)
        many(2, GROUP_STEPS, lambda n: step(n, list(range(GUARD + 8, END + HALO - 8, 8))))

        def copy_out(r):
            there = pl.ds(pl.multiple_of(r + TOP, 8), 8)
            for c in range(RING):
                finish(c, r, state[c, there, :])

        by_rows(copy_out)

    def put_block(out, h, c, rows, value):
        out[0, rows, pl.ds(pl.multiple_of((PART * h + c) * LANES, LANES), LANES)] = value

    def first_part():
        wait_for(send_first + send_corners + send_guess_lanes)
        rows_from(GUARD, TOP, take_beside)
        rows_from(END, END + HALO, take_beside)
        rows_from(GUARD, END + HALO, close_guess)

    def late_part():
        wait_for(send_late)
        rows_from(GUARD + 8, END + 8, take_beside_late)
        by_rows(close_initial)

    def pass_one(h):
        pl.when(h == 0)(first_part)
        pl.when(h == 1)(lambda: wait_for(send_second))
        fine_coefficients(h, GUARD, TOP + 8)
        fine_coefficients(h, END - 8, END + HALO)

        def finish_relaxed(c, r, new):
            rows = pl.ds(r, 8)
            relaxed[h, c, rows, :] = new
            hand[h, c, rows, :] = jnp.where(last, initial[h, c, rows, :], new)
            if c < PART:
                put_block(relaxed_out, h, c, rows, new)

        relax(start.at[0, h], h, finish_relaxed, lambda: wait_for(send_load), late_part)
        pl.when(h == 0)(lambda: act_on(send_relaxed[0], "start", 1))
        pl.when(h == 1)(lambda: act_on(send_relaxed[1], "start", 1))

    many(0, 2, pass_one)

    def put_part(c, rows, inverse, size, sides):
        for d, side in enumerate(sides):
            gedges[d, c, rows, :] = inverse * side
        gscale[c, rows, :] = inverse * size

    def part_coefficients(r):
        coefficients(
            tile(KAPPA, odd), tile(CAP, odd), GROUP_STEPS, inside_part(odd), r, RING, put_part
        )

    rows_from(TOP - NEAR, END + NEAR, part_coefficients)

    wait_for(send_kc)

    chain_inside = jnp.logical_or(
        both(low, jnp.logical_or(me < n_tm - 1, has_right)),
        both(high, jnp.logical_or(me > 0, has_left)),
    )

    def inside_chain(c, r):
        rows = inside_rows(r, CTOP)
        return both(rows, chain_inside) if c else rows

    def put_chain(c, rows, inverse, size, sides):
        for d, side in enumerate(sides):
            cedges[d, c, rows, :] = inverse * side
        cscale[c, rows, :] = inverse * size

    def chain_coefficients(i):
        for u in range(2):
            coefficients(
                lambda c, rows: kc[KAPPA, c, rows, :],
                lambda c, rows: kc[CAP, c, rows, :],
                GROUP_STEPS, inside_chain, pl.multiple_of(GUARD + i * 16 + 8 * u, 8), 2, put_chain,
            )

    many(0, (ROWS + 2 * CHALO) // 16, chain_coefficients)

    def keep_own():
        def body(r):
            for c in range(RING):
                comb[c, pl.ds(pl.multiple_of(r + TOP, 8), 8), :] = residual[0, c, pl.ds(r, 8), :]

        by_rows(body)

    def pass_two(h):
        pl.when(h == 0)(lambda: wait_for(send_relaxed[0]))
        pl.when(h == 1)(lambda: wait_for(send_relaxed[1]))

        def finish_residual(c, r, new):
            rows = pl.ds(r, 8)
            residual[h, c, rows, :] = new - relaxed[h, c, rows, :]
            if c < PART:
                put_block(again_out, h, c, rows, new)

        relax(start.at[1, h], h, finish_residual)
        pl.when(h == 0)(lambda: act_on(send_residual[0], "start", 1))
        pl.when(h == 1)(lambda: act_on(send_residual[1], "start", 1))
        pl.when(both(h == 0, is_even))(keep_own)

    many(0, 2, pass_two)
    for nos in send_residual:
        wait_for(nos)

    def part_base(c, rows, value):
        return gscale[c, rows, :] * value

    solve(gedges, held, part_base, comb, work, list(range(TOP - NEAR, END + NEAR, 8)), RING)

    def fill_box(r):
        rows = pl.ds(r, 8)
        total = []
        for c in range(RING):
            other = jnp.where(is_odd, residual[1, c, rows, :], partner[c, rows, :])
            total.append(comb[c, pl.ds(pl.multiple_of(r + TOP, 8), 8), :] + other)
        for c in range(PART):
            box[c, 0, rows, :] = total[c]
            box[c, 1, rows, :] = jnp.where(low, total[c + 1], total[c - 1])

    by_rows(fill_box)

    def to_chain(src, dst, kind, c, device):
        return pltpu.make_async_remote_copy(
            src_ref=src,
            dst_ref=dst,
            send_sem=a2a_send.at[kind, c],
            recv_sem=a2a_recv.at[kind, pair],
            device_id=device,
            device_id_type=MESH,
        )

    def centre(c):
        t = PART * odd + c
        return to_chain(box.at[c], arrived.at[pair, two, pl.ds(CTOP, ROWS)], 0, c, (t, gx, gy))

    def upward(c, tall):
        return to_chain(
            box.at[c, two, pl.ds(0, tall)], arrived.at[pair, two, pl.ds(CEND, tall)],
            1, c, (PART * odd + c, gx - 1, gy),
        )

    def downward(c, tall):
        return to_chain(
            box.at[c, two, pl.ds(ROWS - tall, tall)],
            arrived.at[pair, two, pl.ds(CTOP - tall, tall)],
            2, c, (PART * odd + c, gx + 1, gy),
        )

    def stay():
        return pltpu.make_async_copy(
            box.at[lax.rem(me, PART)], arrived.at[pair, two, pl.ds(CTOP, ROWS)], local_sem.at[0]
        )

    stays = quarter == odd

    def each(act):
        many(0, PART, act)

    def send_centre(c):
        pl.when(PART * odd + c != me)(lambda: centre(c).start())

    def sent_centre(c):
        pl.when(PART * odd + c != me)(lambda: centre(c).wait_send())

    pl.when(stays)(lambda: stay().start())
    each(send_centre)
    for j in range(n_tm // 2 - 1):
        tall = strip(j)
        pl.when(jnp.logical_and(pair == j, has_up))(
            lambda tall=tall: each(lambda c: upward(c, tall).start())
        )
        pl.when(jnp.logical_and(pair == j, has_down))(
            lambda tall=tall: each(lambda c: downward(c, tall).start())
        )

    def incoming(dst, kind, j):
        return pltpu.make_async_remote_copy(
            src_ref=dst,
            dst_ref=dst,
            send_sem=a2a_send.at[kind, 0],
            recv_sem=a2a_recv.at[kind, j],
            device_id=(me, gx, gy),
            device_id_type=MESH,
        )

    pl.when(stays)(lambda: stay().wait())
    for j in range(n_tm // 2):
        pl.when(2 * j + quarter != me)(
            incoming(arrived.at[j, two, pl.ds(CTOP, ROWS)], 0, j).wait_recv
        )
        if strip(j):
            pl.when(has_down)(incoming(arrived.at[j, two, pl.ds(CEND, strip(j))], 1, j).wait_recv)
            pl.when(has_up)(
                incoming(arrived.at[j, two, pl.ds(CTOP - strip(j), strip(j))], 2, j).wait_recv
            )

    def give_back(k):
        return pltpu.make_async_remote_copy(
            src_ref=out_box.at[k],
            dst_ref=error.at[me],
            send_sem=back_send.at[k],
            recv_sem=back_recv.at[me],
            device_id=(k, gx, gy),
            device_id_type=MESH,
        )

    def keep(k):
        return pltpu.make_async_copy(out_box.at[k], error.at[me], local_sem.at[1])

    def hand_back(k):
        for r in range(0, ROWS, 8):
            out_box[k, pl.ds(r, 8), :] = chain[0, pl.ds(CTOP + r, 8), :]
        pl.when(me == k)(lambda: keep(k).start())
        pl.when(me != k)(lambda: give_back(k).start())

    chain[...] = arrived[0]
    hand_back(1)

    def chain_base(c, rows, value):
        return cscale[c, rows, :] * value

    chain_rows = list(range(GUARD, CEND + CHALO, 8))

    def link(k):
        def add(c, r, new):
            rows = pl.ds(r, 8)
            own = jnp.where(lax.rem(k, 2) == 1, arrived[lax.div(k, 2), c, rows, :], 0.0)
            chain[c, rows, :] = new + own

        solve(cedges, cheld, chain_base, chain, chain_work, chain_rows, 2, add)
        hand_back(k)

    many(2, n_tm, link)

    @pl.when(me == 0)
    def _():
        def fill(t):
            error[t] = jnp.zeros((ROWS, LANES), jnp.float32)

        many(0, n_tm, fill)

    for t in range(n_tm):
        if t:
            pl.when(me == t)(lambda t=t: keep(t).wait())
        pl.when(jnp.logical_and(me != t, me > 0))(
            pltpu.make_async_remote_copy(
                src_ref=error.at[t],
                dst_ref=error.at[t],
                send_sem=back_send.at[t],
                recv_sem=back_recv.at[t],
                device_id=(me, gx, gy),
                device_id_type=MESH,
            ).wait_recv
        )

    def correct(r):
        rows = pl.ds(r, 8)
        for c in range(TILES):
            own = jnp.where(is_even, residual[c // PART, c % PART, rows, :], 0.0)
            error_out[0, rows, columns(c)] = error[c, rows, :] + own

    by_rows(correct)

    act_on(range(len(made)), "wait_send", 1)
    each(sent_centre)
    for j in range(n_tm // 2 - 1):
        tall = strip(j)
        pl.when(jnp.logical_and(pair == j, has_up))(
            lambda tall=tall: each(lambda c: upward(c, tall).wait_send())
        )
        pl.when(jnp.logical_and(pair == j, has_down))(
            lambda tall=tall: each(lambda c: downward(c, tall).wait_send())
        )
    for k in range(1, n_tm):
        pl.when(me != k)(lambda k=k: give_back(k).wait_send())


def shards(sizes, *args):
    f32 = jnp.float32
    vmem = lambda *shape: pltpu.VMEM(shape, f32)
    wide = (RING, TALL, LANES)
    slim = (2, CTALL, LANES)
    flat = (RING, ROWS, LANES)
    block = (ROWS, TILES * LANES)
    in_hbm = pl.BlockSpec(memory_space=pltpu.HBM)
    in_vmem = pl.BlockSpec(memory_space=pltpu.VMEM)
    dma = pltpu.SemaphoreType.DMA
    out = jax.ShapeDtypeStruct((1,) + block, f32)
    relaxed, error, again = pl.pallas_call(
        functools.partial(kernel, sizes),
        out_shape=(out, out, out),
        in_specs=[in_hbm] * 8,
        out_specs=(in_vmem,) * 3,
        scratch_shapes=[
            vmem(4, *block),
            pltpu.VMEM((1 + GROUP_STEPS,) + block, jnp.int32),
            vmem(FIELDS, ALL, TALL, LANES),
            vmem(2, *flat),
            vmem(2, *flat),
            vmem(2, PAIRS, ROWS, LANES),
            vmem(2, PAIRS, TALL, LANES),
            vmem(2, TALL, LANES),
            vmem(2, ROWS, LANES),
            vmem(2, 2, *wide),
            vmem(*wide),
            vmem(*wide),
            vmem(2, 4, *wide),
            vmem(2, *wide),
            vmem(2, *wide),
            vmem(2, *flat),
            vmem(2, *flat),
            vmem(2, *flat),
            vmem(*wide),
            vmem(*flat),
            vmem(4, *wide),
            vmem(*wide),
            vmem(PART, 2, ROWS, LANES),
            vmem(TILES // 2, *slim),
            vmem(2, *slim),
            vmem(2, 2, ROWS, LANES),
            vmem(4, *slim),
            vmem(*slim),
            vmem(*slim),
            vmem(*slim),
            vmem(*slim),
            vmem(TILES, ROWS, LANES),
            vmem(TILES, ROWS, LANES),
            pltpu.SMEM((NCLS,), f32),
            pltpu.SMEM((NLEV,), f32),
            dma((8,)),
            dma((2,)),
            dma((COPIES,)),
            dma((COPIES,)),
            dma((3, PART)),
            dma((3, TILES // 2)),
            dma((TILES,)),
            dma((TILES,)),
        ],
        compiler_params=pltpu.CompilerParams(
            collective_id=0, has_side_effects=True, vmem_limit_bytes=61 * 2**20
        ),
    )(*args)
    return relaxed + error, again - relaxed


def solution(mesh):
    placed = (
        P("gx", "gy"),
        P("tm", "gx", "gy"),
        P("gx", "gy"),
        P(),
        P("gx", "gy"),
        P("gx", "gy"),
        P("tm", "gx", "gy"),
        P(),
    )
    sizes = (mesh.shape["tm"], mesh.shape["gx"], mesh.shape["gy"])
    return jax.shard_map(
        functools.partial(shards, sizes),
        mesh=mesh,
        in_specs=placed,
        out_specs=(P("tm", "gx", "gy"), P("tm", "gx", "gy")),
        check_vma=False,
    )
```

time: 1240 us -> 52.2 us (0.04); the launches traced: 1210 us -> 52.1 us
  starting transfers between devices: 922 us -> 0 us
  waiting for transfers between devices: 237 us -> 0 us
  Pallas kernels: 0 us -> 49.5 us
  other arithmetic: 44.9 us -> 1.96 us
    ppermute x270 -> x0, starting transfers between devices: 922 us -> none  [the longest x130 438 us: with_halo(): lax.ppermute(lax.slice_in_dim(block, block.shape[dim] - width, None, axis...]
    ppermute x270 -> x0, waiting for transfers between devices: 237 us -> none  [the longest x130 151 us: with_halo(): lax.ppermute(lax.slice_in_dim(block, 0, width, axis=dim), axis, backward)]
    pallas_call x0 -> x1, Pallas kernels: none -> 49.5 us  [shards(): pl.pallas_call(functools.partial(kernel, sizes), out_shape=(out, out, out...]
    add x63 -> x0, other arithmetic: 32.1 us -> none  [the longest x55 29.6 us: chebyshev(): newest = weight * (jacobi - previous) + previous]
  transfers between devices with their start and end apart: 270 -> 0, of which waited for: 139 -> 0; matrix products, arithmetic and copies ran while one was open for 0% -> 0% of each run, Pallas kernels for 0% -> 0%
where the time goes in v2:
time: 52.2 us; the launch traced here: 52.1 us
  Pallas kernels  49.5 us (95%)
  other arithmetic  1.96 us (4%)
  between operations  0.64 us (1%)
    pallas_call x1, Pallas kernels, shards(): pl.pallas_call(functools.partial(kernel, sizes), out_shape=(out, out, out...  49.5 us
    sub x1, other arithmetic, shards(): return (relaxed + error, again - relaxed)  1.96 us

profile of v2, /device:TPU:77, one launch (start us, length us, event | category | flops | bytes accessed | tf_op | source)
XLA Modules:
  0.0 52.1 jit_solution(14901844450041133308)
XLA Ops:
  0.6 49.5 %shard_map.95 = (f32[1,64,1024]{2,1,0:T(8,128)}, f32[1,64,1024]{2,1,0:T(8,128)}, f32[1,64,1024]{2,1,0:T(8,128)}) custom-call(f32[64,1024]{1,0:T(8,128)} %initial_hbm.1, f32[1,64,1024]{2,1,0:T(8,128)} %guess_hbm.1, s32[64,1024]{1,0:T(8,128)} %class_hbm.1, f32[8]{0:T(128)} %conductance_hbm.1, f32[64,1024]{1,0:T(8,128)} %cap_hbm.1, f32[64,1024]{1,0:T(8,128)} %base_hbm.1, ...), custom_call_target="tpu_custom_call" | custom-call | tf_op jit(solution)/shard_map/pallas_call | solution.py:801
  50.1 2.0 %fusion = (f32[1,64,1024]{2,1,0:T(8,128)}, f32[1,64,1024]{2,1,0:T(8,128)}) fusion(f32[1,64,1024]{2,1,0:T(8,128)} %get-tuple-element.7, f32[1,64,1024]{2,1,0:T(8,128)} %get-tuple-element.5, f32[1,64,1024]{2,1,0:T(8,128)} %get-tuple-element.6), kind=kLoop, calls=%fused_computation | loop fusion | flops 131072 | bytes 1310720 | tf_op jit(solution)/shard_map/sub | solution.py:855

commit v3 on v2

--- a/solution.py
+++ b/solution.py
@@ -368,15 +368,24 @@
         )
         + to_corners(end_tile, lambda side, rows: guess_beside.at[side, rows], HALO, later)
     )
-    send_first = begin(
-        rows_beside(KAPPA, 3, 0, RING, HALO) + shift_on(guess.at[0], start.at[0, 0], 0, RING)
-    )
-    send_load = begin(rows_beside(LOAD + 1, 1, 0, RING, HALO))
-    send_second = begin(
-        rows_beside(KAPPA, 4, RING, TILES - RING, HALO) + shift_on(guess.at[1], start.at[0, 1], 0, PART)
-    )
+    mine = pl.ds(PART * odd, PART)
+    other = me + 1 - 2 * odd
+    begun = pl.ds(0, 2)
+
+    def fixed(rows):
+        return field.at[begun, mine, rows]
+
+    send_fixed = begin(up_and_down(fixed, fixed, HALO, TOP, me, TOP))
+    send_first = begin(rows_beside(LOAD, 1, 0, RING, HALO) + shift_on(guess.at[0], start.at[0, 0], 0, RING))
+    over, under = pl.ds(GUARD, HALO), pl.ds(END, HALO)
+    forward = [
+        remote(fixed(over), fixed(over), (other, gx, gy), has_up, has_up),
+        remote(fixed(under), fixed(under), (other, gx, gy), has_down, has_down),
+    ]
+    send_load = begin(rows_beside(LOAD + 1, 1, 0, RING, 12))
     send_late = begin(
-        rows_beside(LOAD + 2, 2, 0, TILES, NEAR)
+        rows_beside(LOAD + 2, 1, 0, RING, NEAR)
+        + rows_beside(LOAD + 3, 1, 0, RING, 4)
         + left_and_right(
             lambda side: lane_box.at[side, rest], lambda side: beside.at[side, rest, centre_rows], me
         )
@@ -388,6 +397,13 @@
             lambda side: initial.at[side, 0 if side == 0 else PART - 1],
             lambda side: initial_beside.at[side], me, last, last,
         )
+    )
+    send_second = (
+        rows_beside(LOAD, 1, RING, TILES - RING, HALO)
+        + shift_on(guess.at[1], start.at[0, 1], 0, PART)
+        + rows_beside(LOAD + 1, 1, RING, TILES - RING, 12)
+        + rows_beside(LOAD + 2, 1, RING, TILES - RING, NEAR)
+        + rows_beside(LOAD + 3, 1, RING, TILES - RING, 4)
     )
     two = pl.ds(0, 2)
     send_kc = up_and_down(
@@ -477,7 +493,10 @@
 
     wait_for(send_lanes)
     rows_from(TOP, END, take_beside)
+    wait_for(send_fixed)
+    begin(forward)
     many(0, 2, lambda h: fine_coefficients(h, TOP + 8, END - 8))
+    begin(send_second)
 
     def ring(t):
         return lax.rem(t + ALL, ALL)
@@ -521,7 +540,7 @@
         out[0, rows, pl.ds(pl.multiple_of((PART * h + c) * LANES, LANES), LANES)] = value
 
     def first_part():
-        wait_for(send_first + send_corners + send_guess_lanes)
+        wait_for(forward + send_first + send_corners + send_guess_lanes)
         rows_from(GUARD, TOP, take_beside)
         rows_from(END, END + HALO, take_beside)
         rows_from(GUARD, END + HALO, close_guess)
@@ -849,9 +868,9 @@
             dma((TILES,)),
         ],
         compiler_params=pltpu.CompilerParams(
-            collective_id=0, has_side_effects=True, vmem_limit_bytes=61 * 2**20
+            collective_id=0, has_side_effects=True, vmem_limit_bytes=48 * 2**20
         ),
-    )(*args)
+    )(*[pltpu.with_memory_space_constraint(a, pltpu.HBM) for a in args])
     return relaxed + error, again - relaxed
 
 

time: 52.2 us -> 47.9 us (0.918)
  Pallas kernels: 49.5 us -> 46.1 us
  other arithmetic: 1.96 us -> 0.85 us
    pallas_call x1, Pallas kernels: 49.5 us -> 46.1 us  [shards(): pl.pallas_call(functools.partial(kernel, sizes), out_shape=(out, out, out...]
    sub x1, other arithmetic: 1.96 us -> 0.85 us  [shards(): return (relaxed + error, again - relaxed)]
where the time goes in v3:
time: 47.9 us; the launch traced here: 47.6 us
  Pallas kernels  46.1 us (96%)
  other arithmetic  0.85 us (2%)
  between operations  0.64 us (1%)
    pallas_call x1, Pallas kernels, shards(): pl.pallas_call(functools.partial(kernel, sizes), out_shape=(out, out, out...  46.1 us

profile of v3, /device:TPU:77, one launch (start us, length us, event | category | flops | bytes accessed | tf_op | source)
XLA Modules:
  0.0 47.6 jit_solution(10344290326112321267)
XLA Ops:
  0.6 46.1 %shard_map.95 = (f32[1,64,1024]{2,1,0:T(8,128)S(1)}, f32[1,64,1024]{2,1,0:T(8,128)S(1)}, f32[1,64,1024]{2,1,0:T(8,128)S(1)}) custom-call(f32[64,1024]{1,0:T(8,128)} %initial_hbm.1, f32[1,64,1024]{2,1,0:T(8,128)} %guess_hbm.1, s32[64,1024]{1,0:T(8,128)} %class_hbm.1, f32[8]{0:T(128)} %conductance_hbm.1, f32[64,1024]{1,0:T(8,128)} %cap_hbm.1, ...), custom_call_target="tpu_custom_call" | custom-call | tf_op jit(solution)/shard_map/pallas_call | solution.py:820
  46.8 0.8 %fusion = (f32[1,64,1024]{2,1,0:T(8,128)}, f32[1,64,1024]{2,1,0:T(8,128)}) fusion(f32[1,64,1024]{2,1,0:T(8,128)S(1)} %get-tuple-element.7, f32[1,64,1024]{2,1,0:T(8,128)S(1)} %get-tuple-element.5, f32[1,64,1024]{2,1,0:T(8,128)S(1)} %get-tuple-element.6), kind=kLoop, calls=%fused_computation | loop fusion | flops 131072 | bytes 1310720 | tf_op jit(solution)/shard_map/sub | solution.py:874

commit v4 on v3

--- a/solution.py
+++ b/solution.py
@@ -171,6 +171,10 @@
 
     def by_rows(body):
         rows_from(0, ROWS, body)
+
+    def spread(lo, hi, body):
+        for r in range(lo, hi, 8):
+            body(r)
 
     def columns(c):
         return slice(c * LANES, (c + 1) * LANES)
@@ -351,23 +355,6 @@
 
     every = pl.ds(0, ROWS)
     early, rest = pl.ds(0, 2), pl.ds(2, 1)
-    send_lanes = begin(
-        left_and_right(
-            lambda side: lane_box.at[side, early], lambda side: beside.at[side, early, centre_rows], me
-        )
-    )
-    send_guess_lanes = begin(
-        left_and_right(
-            lambda side: end_tile(side, every), lambda side: guess_beside.at[side, centre_rows], later
-        )
-    )
-    send_corners = begin(
-        to_corners(
-            lambda side, rows: lane_box.at[side, early, rows],
-            lambda side, rows: beside.at[side, early, rows], HALO, me,
-        )
-        + to_corners(end_tile, lambda side, rows: guess_beside.at[side, rows], HALO, later)
-    )
     mine = pl.ds(PART * odd, PART)
     other = me + 1 - 2 * odd
     begun = pl.ds(0, 2)
@@ -382,6 +369,23 @@
         remote(fixed(over), fixed(over), (other, gx, gy), has_up, has_up),
         remote(fixed(under), fixed(under), (other, gx, gy), has_down, has_down),
     ]
+    send_lanes = begin(
+        left_and_right(
+            lambda side: lane_box.at[side, early], lambda side: beside.at[side, early, centre_rows], me
+        )
+    )
+    send_guess_lanes = begin(
+        left_and_right(
+            lambda side: end_tile(side, every), lambda side: guess_beside.at[side, centre_rows], later
+        )
+    )
+    send_corners = begin(
+        to_corners(
+            lambda side, rows: lane_box.at[side, early, rows],
+            lambda side, rows: beside.at[side, early, rows], HALO, me,
+        )
+        + to_corners(end_tile, lambda side, rows: guess_beside.at[side, rows], HALO, later)
+    )
     send_load = begin(rows_beside(LOAD + 1, 1, 0, RING, 12))
     send_late = begin(
         rows_beside(LOAD + 2, 1, 0, RING, NEAR)
@@ -489,10 +493,10 @@
         def body(r):
             coefficients(tile(KAPPA, h), tile(CAP, h), 1, inside_part(h), r, RING, put)
 
-        rows_from(lo, hi, body)
+        spread(lo, hi, body)
 
     wait_for(send_lanes)
-    rows_from(TOP, END, take_beside)
+    spread(TOP, END, take_beside)
     wait_for(send_fixed)
     begin(forward)
     many(0, 2, lambda h: fine_coefficients(h, TOP + 8, END - 8))
@@ -510,7 +514,6 @@
             kc_box[f, 1, rows, :] = wide
             kc[f, 0, pl.ds(CTOP + r, 8), :] = own
             kc[f, 1, pl.ds(CTOP + r, 8), :] = wide
-    begin(send_kc)
 
     def relax(state, h, finish, second=None, third=None):
         def step(n, rows_of):
@@ -530,29 +533,33 @@
         many(2, GROUP_STEPS, lambda n: step(n, list(range(GUARD + 8, END + HALO - 8, 8))))
 
         def copy_out(r):
-            there = pl.ds(pl.multiple_of(r + TOP, 8), 8)
             for c in range(RING):
-                finish(c, r, state[c, there, :])
-
-        by_rows(copy_out)
+                finish(c, r, state[c, pl.ds(r + TOP, 8), :])
+
+        spread(0, ROWS, copy_out)
 
     def put_block(out, h, c, rows, value):
         out[0, rows, pl.ds(pl.multiple_of((PART * h + c) * LANES, LANES), LANES)] = value
 
     def first_part():
         wait_for(forward + send_first + send_corners + send_guess_lanes)
-        rows_from(GUARD, TOP, take_beside)
-        rows_from(END, END + HALO, take_beside)
-        rows_from(GUARD, END + HALO, close_guess)
+        spread(GUARD, TOP, take_beside)
+        spread(END, END + HALO, take_beside)
+        spread(GUARD, END + HALO, close_guess)
 
     def late_part():
         wait_for(send_late)
-        rows_from(GUARD + 8, END + 8, take_beside_late)
-        by_rows(close_initial)
+        spread(GUARD + 8, END + 8, take_beside_late)
+        spread(0, ROWS, close_initial)
 
     def pass_one(h):
         pl.when(h == 0)(first_part)
-        pl.when(h == 1)(lambda: wait_for(send_second))
+
+        @pl.when(h == 1)
+        def _():
+            begin(send_kc)
+            wait_for(send_second)
+
         fine_coefficients(h, GUARD, TOP + 8)
         fine_coefficients(h, END - 8, END + HALO)
 
@@ -610,9 +617,9 @@
     def keep_own():
         def body(r):
             for c in range(RING):
-                comb[c, pl.ds(pl.multiple_of(r + TOP, 8), 8), :] = residual[0, c, pl.ds(r, 8), :]
-
-        by_rows(body)
+                comb[c, pl.ds(r + TOP, 8), :] = residual[0, c, pl.ds(r, 8), :]
+
+        spread(0, ROWS, body)
 
     def pass_two(h):
         pl.when(h == 0)(lambda: wait_for(send_relaxed[0]))
@@ -643,12 +650,12 @@
         total = []
         for c in range(RING):
             other = jnp.where(is_odd, residual[1, c, rows, :], partner[c, rows, :])
-            total.append(comb[c, pl.ds(pl.multiple_of(r + TOP, 8), 8), :] + other)
+            total.append(comb[c, pl.ds(r + TOP, 8), :] + other)
         for c in range(PART):
             box[c, 0, rows, :] = total[c]
             box[c, 1, rows, :] = jnp.where(low, total[c + 1], total[c - 1])
 
-    by_rows(fill_box)
+    spread(0, ROWS, fill_box)
 
     def to_chain(src, dst, kind, c, device):
         return pltpu.make_async_remote_copy(
@@ -750,9 +757,10 @@
     def chain_base(c, rows, value):
         return cscale[c, rows, :] * value
 
-    chain_rows = list(range(GUARD, CEND + CHALO, 8))
-
-    def link(k):
+
+    def link(k, beside_rows):
+        chain_rows = list(range(CTOP - beside_rows, CEND + beside_rows, 8))
+
         def add(c, r, new):
             rows = pl.ds(r, 8)
             own = jnp.where(lax.rem(k, 2) == 1, arrived[lax.div(k, 2), c, rows, :], 0.0)
@@ -761,7 +769,9 @@
         solve(cedges, cheld, chain_base, chain, chain_work, chain_rows, 2, add)
         hand_back(k)
 
-    many(2, n_tm, link)
+    many(2, 4, lambda k: link(k, 24))
+    many(4, 6, lambda k: link(k, 16))
+    many(6, n_tm, lambda k: link(k, 8))
 
     @pl.when(me == 0)
     def _():
@@ -790,7 +800,7 @@
             own = jnp.where(is_even, residual[c // PART, c % PART, rows, :], 0.0)
             error_out[0, rows, columns(c)] = error[c, rows, :] + own
 
-    by_rows(correct)
+    spread(0, ROWS, correct)
 
     act_on(range(len(made)), "wait_send", 1)
     each(sent_centre)

time: 47.9 us -> 45.8 us (0.956)
  Pallas kernels: 46.1 us -> 44.2 us
    pallas_call x1, Pallas kernels: 46.1 us -> 44.2 us  [shards(): pl.pallas_call(functools.partial(kernel, sizes), out_shape=(out, out, out...]
where the time goes in v4:
time: 45.8 us; the launch traced here: 45.7 us
  Pallas kernels  44.2 us (97%)
  other arithmetic  0.85 us (2%)
  between operations  0.64 us (1%)
    pallas_call x1, Pallas kernels, shards(): pl.pallas_call(functools.partial(kernel, sizes), out_shape=(out, out, out...  44.2 us

profile of v4, /device:TPU:77, one launch (start us, length us, event | category | flops | bytes accessed | tf_op | source)
XLA Modules:
  0.0 45.7 jit_solution(496743583591518776)
XLA Ops:
  0.6 44.2 %shard_map.95 = (f32[1,64,1024]{2,1,0:T(8,128)S(1)}, f32[1,64,1024]{2,1,0:T(8,128)S(1)}, f32[1,64,1024]{2,1,0:T(8,128)S(1)}) custom-call(f32[64,1024]{1,0:T(8,128)} %initial_hbm.1, f32[1,64,1024]{2,1,0:T(8,128)} %guess_hbm.1, s32[64,1024]{1,0:T(8,128)} %class_hbm.1, f32[8]{0:T(128)} %conductance_hbm.1, f32[64,1024]{1,0:T(8,128)} %cap_hbm.1, ...), custom_call_target="tpu_custom_call" | custom-call | tf_op jit(solution)/shard_map/pallas_call | solution.py:830
  44.9 0.8 %fusion = (f32[1,64,1024]{2,1,0:T(8,128)}, f32[1,64,1024]{2,1,0:T(8,128)}) fusion(f32[1,64,1024]{2,1,0:T(8,128)S(1)} %get-tuple-element.7, f32[1,64,1024]{2,1,0:T(8,128)S(1)} %get-tuple-element.5, f32[1,64,1024]{2,1,0:T(8,128)S(1)} %get-tuple-element.6), kind=kLoop, calls=%fused_computation | loop fusion | flops 131072 | bytes 1310720 | tf_op jit(solution)/shard_map/sub | solution.py:884

commit v5 on v4

--- a/solution.py
+++ b/solution.py
@@ -495,10 +495,10 @@
 
         spread(lo, hi, body)
 
+    wait_for(send_fixed)
+    begin(forward)
     wait_for(send_lanes)
     spread(TOP, END, take_beside)
-    wait_for(send_fixed)
-    begin(forward)
     many(0, 2, lambda h: fine_coefficients(h, TOP + 8, END - 8))
     begin(send_second)
 

time: 45.8 us -> 45.8 us (level)
  no operation moved by 1% of the time
where the time goes in v5:
time: 45.8 us; the launch traced here: 45.7 us
  Pallas kernels  44.2 us (97%)
  other arithmetic  0.85 us (2%)
  between operations  0.64 us (1%)
    pallas_call x1, Pallas kernels, shards(): pl.pallas_call(functools.partial(kernel, sizes), out_shape=(out, out, out...  44.2 us

profile of v5, /device:TPU:77, one launch (start us, length us, event | category | flops | bytes accessed | tf_op | source)
XLA Modules:
  0.0 45.7 jit_solution(6236393425190814950)
XLA Ops:
  0.6 44.2 %shard_map.95 = (f32[1,64,1024]{2,1,0:T(8,128)S(1)}, f32[1,64,1024]{2,1,0:T(8,128)S(1)}, f32[1,64,1024]{2,1,0:T(8,128)S(1)}) custom-call(f32[64,1024]{1,0:T(8,128)} %initial_hbm.1, f32[1,64,1024]{2,1,0:T(8,128)} %guess_hbm.1, s32[64,1024]{1,0:T(8,128)} %class_hbm.1, f32[8]{0:T(128)} %conductance_hbm.1, f32[64,1024]{1,0:T(8,128)} %cap_hbm.1, ...), custom_call_target="tpu_custom_call" | custom-call | tf_op jit(solution)/shard_map/pallas_call | solution.py:830
  44.9 0.8 %fusion = (f32[1,64,1024]{2,1,0:T(8,128)}, f32[1,64,1024]{2,1,0:T(8,128)}) fusion(f32[1,64,1024]{2,1,0:T(8,128)S(1)} %get-tuple-element.7, f32[1,64,1024]{2,1,0:T(8,128)S(1)} %get-tuple-element.5, f32[1,64,1024]{2,1,0:T(8,128)S(1)} %get-tuple-element.6), kind=kLoop, calls=%fused_computation | loop fusion | flops 131072 | bytes 1310720 | tf_op jit(solution)/shard_map/sub | solution.py:884
